TPU v7x, 128 devices: a whole 4x4x4 slice. The times are simulated.
128 devices in a mesh: tm: 32 (over x_lo, z, y), guide: 4 (over x_hi, core).
Axes of the slice: x: 4 (x_hi: 2, x_lo: 2; x = x_hi * 2 + x_lo), y: 4, z: 4, core: 2. Of those that a mesh axis runs over, the one named last changes fastest.
Arguments:
- hidden_rows: bfloat16 [4, 24576, 1024], P('guide', 'tm'), may hold values from -6 to 6
- modulation: float32 [4, 3, 1024], P('guide'), may hold values from -3 to 3
- project_in: bfloat16 [1024, 3072], replicated, may hold values from -0.1875 to 0.1875
- project_out: bfloat16 [1024, 1024], replicated, may hold values from -0.1875 to 0.1875
- to_vocoder: bfloat16 [1024, 384], replicated, may hold values from -0.1875 to 0.1875
- upsample_taps: bfloat16 [4, 384, 192], replicated, may hold values from -0.21875 to 0.21875
- snake_alpha: float32 [192], replicated, may hold values from 0.2 to 3
- guidance: float32 [2], replicated, may hold values from 1 to 3
- branch_ids: int32 [4], replicated, may hold values from 0 to 1, as said below
Outputs:
- wave_features: bfloat16 [384, 49152], P('guide', 'tm')
Inputs may be any that keep to these rules, and one draw needn't show every extreme that they name: `branch_ids`: rows 2s and 2s + 1 hold one 0 and one 1, for every stream s.
All inputs are finite; a program needn't handle non-finite values.
Results may differ from a plain program's by a relative error of at most 0.015.
Values may be sent and summed in bfloat16 or wider, within the bound.
A program may use at most 128 MiB of HBM per device.

v0:
```python
import math

import jax
import jax.numpy as jnp
from jax import lax
from jax.sharding import PartitionSpec as P

HEADS = 16
BLOCK = 48


HALF_BAND = (3.0 / 256.0, -25.0 / 256.0, 150.0 / 256.0, 150.0 / 256.0, -25.0 / 256.0, 3.0 / 256.0)
LOW_PASS = (0.012, -0.06, 0.3, 0.3, -0.06, 0.012)
CENTER_TAP = 0.5


def padded(block, sides, width):
    for axis, dim in sides:
        count = lax.axis_size(axis)
        forward = [(i, i + 1) for i in range(count - 1)]
        backward = [(target, source) for source, target in forward]
        low = lax.ppermute(
            lax.slice_in_dim(block, block.shape[dim] - width, None, axis=dim), axis, forward
        )
        high = lax.ppermute(lax.slice_in_dim(block, 0, width, axis=dim), axis, backward)
        block = jnp.concatenate([low, block, high], axis=dim)
    return block


def partner_2(block, axis, stride):
    count = lax.axis_size(axis)
    route = []
    for low in range(count):
        high = low | 1 << stride
        if high != low and high < count:
            route += [(low, high), (high, low)]
    return lax.ppermute(block, axis, route)


def modulated(rows_in, scale_row, shift_row):
    widened = rows_in.astype(jnp.float32)
    centered = widened - jnp.mean(widened, axis=-1, keepdims=True)
    variance = jnp.mean(centered * centered, axis=-1, keepdims=True)
    normed = centered * lax.rsqrt(variance + 1e-06)
    return (normed * (1.0 + scale_row) + shift_row).astype(jnp.bfloat16)


def block_attend(queries, extended, usable, head_count, block):
    frames = queries.shape[0]
    model_width = queries.shape[1]
    head_size = model_width // head_count
    count = frames // block
    query_blocks = queries.reshape(count, block, head_count, head_size)
    pieces = [
        extended[j * block : j * block + frames].reshape(count, block, 2 * model_width)
        for j in range(4)
    ]
    key_rows = jnp.concatenate(pieces, axis=1)
    key_heads = key_rows[:, :, :model_width].reshape(count, 4 * block, head_count, head_size)
    value_heads = key_rows[:, :, model_width:].reshape(count, 4 * block, head_count, head_size)
    scores = jnp.einsum(
        "nqhd,nkhd->nhqk", query_blocks, key_heads, preferred_element_type=jnp.float32
    )
    scores = scores * (1.0 / math.sqrt(head_size))
    scores = jnp.where(usable[:, None, None, :], scores, -jnp.inf)
    row_max = jnp.max(scores, axis=3, keepdims=True)
    raised = jnp.exp(scores - row_max)
    weights = (raised / jnp.sum(raised, axis=3, keepdims=True)).astype(jnp.bfloat16)
    result = jnp.einsum("nhqk,nkhd->nqhd", weights, value_heads, preferred_element_type=jnp.float32)
    return result.astype(jnp.bfloat16).reshape(frames, model_width)


def channel_mix(weight, signal):
    return lax.dot_general(
        weight, signal, (((0,), (0,)), ((), ())), preferred_element_type=jnp.float32
    )


def upsample(window, tap_table):
    span = window.shape[1] - 2
    even_part = channel_mix(tap_table[1], window[:, 1 : span + 1]) + channel_mix(
        tap_table[3], window[:, 0:span]
    )
    odd_part = channel_mix(tap_table[0], window[:, 2 : span + 2]) + channel_mix(
        tap_table[2], window[:, 1 : span + 1]
    )
    return jnp.stack([even_part, odd_part], axis=2).reshape(even_part.shape[0], 2 * span)


def periodic(values, snake_rate):
    return values + jnp.square(jnp.sin(snake_rate * values)) / snake_rate


def activate(extended, snake_rate, odd_usable):
    span = extended.shape[1] - 10
    odd_edge = HALF_BAND[0] * extended[:, 0 : span + 5]
    for offset in range(1, 6):
        odd_edge = odd_edge + HALF_BAND[offset] * extended[:, offset : offset + span + 5]
    odd_edge = jnp.where(odd_usable[None, :], periodic(odd_edge, snake_rate), 0.0)
    result = CENTER_TAP * periodic(extended[:, 5 : 5 + span], snake_rate)
    for offset in range(6):
        result = result + LOW_PASS[offset] * odd_edge[:, offset : offset + span]
    return result


def on_device(
    hidden_rows,
    modulation,
    project_in,
    project_out,
    to_vocoder,
    upsample_taps,
    snake_alpha,
    guidance,
    branch_ids,
):
    chain_len = lax.axis_size("tm")
    position = lax.axis_index("tm")
    member = lax.axis_index("guide")
    rows_in = hidden_rows[0]
    frames = rows_in.shape[0]
    model_width = rows_in.shape[1]
    normed = modulated(rows_in, modulation[0, 0], modulation[0, 1])
    projections = jnp.dot(normed, project_in, preferred_element_type=jnp.float32).astype(
        jnp.bfloat16
    )
    queries = projections[:, :model_width]
    key_value = projections[:, model_width:]
    rimmed = padded(key_value, (("tm", 0),), 2 * BLOCK)
    extended = rimmed[: frames + 3 * BLOCK]
    local_blocks = frames // BLOCK
    block_ids = position * local_blocks + jnp.arange(local_blocks, dtype=jnp.int32)
    key_ids = block_ids[:, None] - 2 + (jnp.arange(4 * BLOCK, dtype=jnp.int32) // BLOCK)[None, :]
    usable = (key_ids >= 0) & (key_ids < chain_len * local_blocks)
    attended = block_attend(queries, extended, usable, HEADS, BLOCK)
    mixed_out = jnp.dot(attended, project_out, preferred_element_type=jnp.float32)
    updated = (rows_in.astype(jnp.float32) + modulation[0, 2] * mixed_out).astype(jnp.bfloat16)
    projected = lax.dot_general(
        to_vocoder, updated, (((0,), (1,)), ((), ())), preferred_element_type=jnp.float32
    )
    partner = partner_2(projected.astype(jnp.bfloat16), "guide", 0).astype(projected.dtype)
    own_branch = jnp.sum(
        jnp.where(jnp.arange(branch_ids.shape[0], dtype=jnp.int32) == member, branch_ids, 0)
    )
    guide_scale = jnp.sum(
        jnp.where(jnp.arange(guidance.shape[0], dtype=jnp.int32) == member // 2, guidance, 0.0)
    )
    cond_rows = jnp.where(own_branch == 0, projected, partner)
    uncond_rows = jnp.where(own_branch == 0, partner, projected)
    guided = (uncond_rows + guide_scale * (cond_rows - uncond_rows)).astype(jnp.bfloat16)
    half_out = upsample_taps.shape[2] // 2
    parity = member % 2
    tap_table = lax.dynamic_slice_in_dim(upsample_taps, parity * half_out, half_out, 2)
    snake_rate = lax.dynamic_slice_in_dim(snake_alpha, parity * half_out, half_out, 0)[:, None]
    length = 2 * frames
    all_frames = length * chain_len
    local_index = jnp.arange(length + 5, dtype=jnp.int32) - 3 + position * length
    odd_usable = (local_index >= 0) & (local_index < all_frames)
    with_rim = padded(guided, (("tm", 1),), 1)
    inner = upsample(with_rim, tap_table)
    upsampled = padded(inner.astype(jnp.bfloat16), (("tm", 1),), 5).astype(inner.dtype)
    return activate(upsampled, snake_rate, odd_usable).astype(jnp.bfloat16)


def solution(mesh):
    in_specs = (P("guide", "tm", None), P("guide", None, None), P(), P(), P(), P(), P(), P(), P())
    out_specs = P("guide", "tm")
    return jax.shard_map(
        on_device, mesh=mesh, in_specs=in_specs, out_specs=out_specs, check_vma=False
    )
```

profile of v0, /device:TPU:7, one launch (start us, length us, event | category | flops | bytes accessed | tf_op | source)
XLA Modules:
  0.0 146.3 jit_solution(16552959763121361134)
XLA Ops:
  0.9 1.8 %convert_reduce_fusion = f32[768]{0:T(1024)S(1)} fusion(bf16[1,768,1024]{2,1,0:T(8,128)(2,1)} %param.9), kind=kLoop, calls=%fused_computation.11 | loop fusion | flops 1572096 | bytes 1575936 | tf_op jit(solution)/shard_map/reduce_sum | solution.py:42
  2.7 2.0 %fusion.11 = f32[768]{0:T(1024)S(1)} fusion(bf16[1,768,1024]{2,1,0:T(8,128)(2,1)} %param.9, f32[768]{0:T(1024)S(1)} %broadcast_multiply_fusion), kind=kLoop, calls=%fused_computation.20 | loop fusion | flops 3144960 | bytes 1579008 | tf_op jit(solution)/shard_map/reduce_sum | solution.py:43
  4.6 8.4 %convolution_convert_fusion = bf16[768,3072]{1,0:T(8,128)(2,1)S(1)} fusion(bf16[1024,3072]{1,0:T(8,128)(2,1)} %param.11, bf16[1,768,1024]{2,1,0:T(8,128)(2,1)S(1)} %copy-done.2, f32[1024]{0:T(1024)S(1)} %bitcast.74, f32[1024]{0:T(1024)S(1)} %bitcast.75, f32[768]{0:T(1024)S(1)} %add_rsqrt_fusion, f32[768]{0:T(1024)S(1)} %broadcast_multiply_fusion), kind=kOutput, calls=%fused_computation.10 | convolution fusion | flops 4838916096 | bytes 12597248 | tf_op jit(solution)/shard_map/dot_general | solution.py:124
  13.9 3.2 %collective-permute-start = (bf16[96,2048]{1,0:T(8,128)(2,1)}, bf16[96,2048]{1,0:T(8,128)(2,1)S(1)}, u32[]{:S(2)}, u32[]{:S(2)}) collective-permute-start(bf16[96,2048]{1,0:T(8,128)(2,1)} %get-tuple-element.7), channel_id=1, source_target_pairs={{0,4},{4,8},{8,12},{12,16},{16,20},{20,24},{24,28},{28,32},{32,36}... | collective-permute-start | bytes 1179656 | tf_op jit(solution)/shard_map/ppermute | solution.py:22
  17.1 7.3 %collective-permute-start.1 = (bf16[96,2048]{1,0:T(8,128)(2,1)S(1)}, bf16[96,2048]{1,0:T(8,128)(2,1)S(1)}, u32[]{:S(2)}, u32[]{:S(2)}) collective-permute-start(bf16[96,2048]{1,0:T(8,128)(2,1)S(1)} %get-tuple-element.8), channel_id=1, source_target_pairs={{4,0},{8,4},{12,8},{16,12},{20,16},{24,20},{28,24},{32,28},{36,32}... | collective-permute-start | bytes 1179656 | tf_op jit(solution)/shard_map/ppermute | solution.py:25
  24.4 2.0 %slice.154 = bf16[768,2048]{1,0:T(8,128)(2,1)} slice(bf16[768,3072]{1,0:T(8,128)(2,1)S(1)} %convolution_convert_fusion), slice={[0:768], [1024:3072]} | slice | bytes 6291456 | tf_op jit(solution)/shard_map/slice | solution.py:128
  27.6 5.3 %reshape.109 = bf16[16,48,16,64]{3,2,1,0:T(8,128)(2,1)} reshape(bf16[768,1024]{1,0:T(8,128)(2,1)} %slice.159) | data formatting | bytes 3145728 | tf_op jit(solution)/shard_map/reshape | solution.py:53
  32.9 4.7 %fusion.10 = (bf16[768,2048]{1,0:T(8,128)(2,1)S(1)}, bf16[768,2048]{1,0:T(8,128)(2,1)S(1)}, bf16[768,2048]{1,0:T(8,128)(2,1)S(1)}) fusion(bf16[96,2048]{1,0:T(8,128)(2,1)S(1)} %collective-permute-done, bf16[768,2048]{1,0:T(8,128)(2,1)} %slice.154, bf16[96,2048]{1,0:T(8,128)(2,1)S(1)} %collective-permute-done.1), kind=kLoop, calls=%fused_computation.19 | loop fusion | flops 18874368 | bytes 13369344 | tf_op jit(solution)/shard_map/concatenate | solution.py:26
  39.1 5.2 %fusion.61 = (bf16[16,192,1024]{2,1,0:T(8,128)(2,1)}, bf16[16,192,1024]{2,1,0:T(8,128)(2,1)}) fusion(bf16[16,192,2048]{2,1,0:T(8,128)(2,1)S(1)} %pad_maximum_fusion), kind=kLoop, calls=%fused_computation.110 | loop fusion | bytes 25165824 | tf_op jit(solution)/shard_map/slice | solution.py:59
  44.4 11.0 %copy.14 = bf16[16,192,1024]{1,2,0:T(8,128)(2,1)} copy(bf16[16,192,1024]{2,1,0:T(8,128)(2,1)} %get-tuple-element.5) | data formatting | bytes 12582912 | tf_op jit(solution)/shard_map/slice | solution.py:59
  55.4 11.1 %copy.13 = bf16[16,192,1024]{1,2,0:T(8,128)(2,1)} copy(bf16[16,192,1024]{2,1,0:T(8,128)(2,1)} %get-tuple-element.6) | data formatting | bytes 12582912 | tf_op jit(solution)/shard_map/slice | solution.py:60
  66.5 6.1 %fusion.16 = f32[16,16,48,192]{3,2,1,0:T(8,128)S(1)} fusion(bf16[16,192,16,64]{1,3,2,0:T(8,128)(2,1)} %bitcast.65, bf16[16,48,16,64]{3,2,1,0:T(8,128)(2,1)} %reshape.109), kind=kOutput, calls=%fused_computation.27 | convolution fusion | flops 301989888 | bytes 17301504 | tf_op jit(solution)/shard_map/nqhd,nkhd->nhqk/dot_general | solution.py:61
  72.6 6.9 %fusion.66 = (f32[16,16,48]{2,1,0:T(8,128)S(1)}, f32[16,16,48,192]{3,2,1,0:T(8,128)}) fusion(f32[16,16,48,192]{3,2,1,0:T(8,128)S(1)} %fusion.16, pred[16,192]{1,0:T(8,128)(4,1)S(1)} %fusion.47), kind=kOutput, calls=%fused_computation.115 | output fusion | flops 14155967 | bytes 18926592 | tf_op jit(solution)/shard_map/sub | solution.py:67
  79.5 11.5 %convert_bitcast_fusion.1 = bf16[16,48,16,64]{3,1,2,0:T(8,128)(2,1)} fusion(bf16[16,192,16,64]{1,3,2,0:T(8,128)(2,1)} %bitcast.70, f32[16,16,48,192]{3,2,1,0:T(8,128)} %get-tuple-element.20, f32[16,16,48]{2,1,0:T(8,128)S(1)} %get-tuple-element.19), kind=kOutput, calls=%fused_computation.29 | convolution fusion | flops 307494912 | bytes 17350656 | tf_op jit(solution)/shard_map/nhqk,nkhd->nqhd/dot_general | solution.py:69
  91.0 4.4 %copy.16 = bf16[16,48,16,64]{3,2,1,0:T(8,128)(2,1)} copy(bf16[16,48,16,64]{3,1,2,0:T(8,128)(2,1)} %convert_bitcast_fusion.1) | data formatting | bytes 3145728 | tf_op jit(solution)/shard_map/convert_element_type | solution.py:70
  95.3 5.4 %reshape.111 = bf16[768,1024]{1,0:T(8,128)(2,1)} reshape(bf16[16,48,16,64]{3,2,1,0:T(8,128)(2,1)} %copy.16) | data formatting | bytes 3145728 | tf_op jit(solution)/shard_map/reshape | solution.py:70
  100.7 5.5 %fusion.67 = (bf16[384,768]{0,1:T(8,128)(2,1)}, f32[384,768]{0,1:T(8,128)S(1)}) fusion(bf16[1024,384]{1,0:T(8,128)(2,1)} %param.13, bf16[1,768,1024]{2,1,0:T(8,128)(2,1)} %param.9, bf16[768,1024]{1,0:T(8,128)(2,1)} %reshape.111, bf16[1024,1024]{1,0:T(8,128)(2,1)S(1)} %copy-done, f32[1024]{0:T(1024)S(1)} %bitcast.73), kind=kOutput, calls=%fused_computation.116 | convolution fusion | flops 2218033152 | bytes 7802880 | tf_op jit(solution)/shard_map/dot_general | solution.py:138
  109.2 2.0 %fusion.26 = bf16[384,768]{0,1:T(8,128)(2,1)S(1)} fusion(f32[384,768]{0,1:T(8,128)S(1)} %get-tuple-element.22, bf16[384,768]{0,1:T(8,128)(2,1)} %collective-permute-done.2, f32[]{:T(128)} %fusion.56, pred[]{:T(512)S(6)} %eq.20), kind=kLoop, calls=%fused_computation.40 | loop fusion | flops 2064384 | bytes 2359301 | tf_op jit(solution)/shard_map/convert_element_type | solution.py:150
  111.2 1.9 %collective-permute-start.3 = (bf16[384,1]{0,1:T(2,128)(2,1)S(1)}, bf16[384,1]{0,1:T(2,128)(2,1)S(1)}, u32[]{:S(2)}, u32[]{:S(2)}) collective-permute-start(bf16[384,1]{0,1:T(2,128)(2,1)S(1)} %get-tuple-element.12), channel_id=1, source_target_pairs={{0,4},{4,8},{8,12},{12,16},{16,20},{20,24},{24,28},{28,32},{32,36}... | collective-permute-start | bytes 2312 | tf_op jit(solution)/shard_map/ppermute | solution.py:22
  113.1 7.9 %collective-permute-start.4 = (bf16[384,1]{0,1:T(2,128)(2,1)S(1)}, bf16[384,1]{0,1:T(2,128)(2,1)S(1)}, u32[]{:S(2)}, u32[]{:S(2)}) collective-permute-start(bf16[384,1]{0,1:T(2,128)(2,1)S(1)} %get-tuple-element.13), channel_id=1, source_target_pairs={{4,0},{8,4},{12,8},{16,12},{20,16},{24,20},{28,24},{32,28},{36,32}... | collective-permute-start | bytes 2312 | tf_op jit(solution)/shard_map/ppermute | solution.py:25
  126.4 1.9 %collective-permute-start.5 = (bf16[96,5]{0,1:T(8,128)(2,1)S(1)}, bf16[96,5]{0,1:T(8,128)(2,1)S(1)}, u32[]{:S(2)}, u32[]{:S(2)}) collective-permute-start(bf16[96,5]{0,1:T(8,128)(2,1)S(1)} %get-tuple-element.15), channel_id=1, source_target_pairs={{0,4},{4,8},{8,12},{12,16},{16,20},{20,24},{24,28},{28,32},{32,36}... | collective-permute-start | bytes 2888 | tf_op jit(solution)/shard_map/ppermute | solution.py:22
  128.3 7.6 %collective-permute-start.6 = (bf16[96,5]{0,1:T(8,128)(2,1)S(1)}, bf16[96,5]{0,1:T(8,128)(2,1)S(1)}, u32[]{:S(2)}, u32[]{:S(2)}) collective-permute-start(bf16[96,5]{0,1:T(8,128)(2,1)S(1)} %get-tuple-element.14), channel_id=1, source_target_pairs={{4,0},{8,4},{12,8},{16,12},{20,16},{24,20},{28,24},{32,28},{36,32}... | collective-permute-start | bytes 2888 | tf_op jit(solution)/shard_map/ppermute | solution.py:25
  138.0 4.1 %add_select_fusion = f32[96,1541]{0,1:T(8,128)S(1)} fusion(f32[96,1546]{0,1:T(8,128)S(1)} %convert_element_type.56, f32[96]{0:T(128)S(1)} %dynamic_slice.7, pred[1541]{0:T(1024)(128)(4,1)S(1)} %fusion.50), kind=kLoop, calls=%fused_computation.58 | loop fusion | flops 2366976 | bytes 4144133 | tf_op jit(solution)/shard_map/jit(_where)/select_n | solution.py:99
  142.1 3.4 %fusion.37 = bf16[96,1536]{0,1:T(8,128)(2,1)S(1)} fusion(f32[96,1541]{0,1:T(8,128)S(1)} %add_select_fusion, f32[96,1546]{0,1:T(8,128)S(1)} %convert_element_type.56, f32[96]{0:T(128)S(1)} %dynamic_slice.7), kind=kLoop, calls=%fused_computation.61 | loop fusion | flops 2654208 | bytes 4424064 | tf_op jit(solution)/shard_map/convert_element_type | solution.py:162
  (44 shorter events, 15.1 us)
Async XLA Ops:
  0.0 100.7 %copy-start = (bf16[1024,1024]{1,0:T(8,128)(2,1)S(1)}, bf16[1024,1024]{1,0:T(8,128)(2,1)}, u32[]{:S(2)}) copy-start(bf16[1024,1024]{1,0:T(8,128)(2,1)} %param.12) | copy-start | bytes 6291460
  0.0 4.6 %copy-start.2 = (bf16[1,768,1024]{2,1,0:T(8,128)(2,1)S(1)}, bf16[1,768,1024]{2,1,0:T(8,128)(2,1)}, u32[]{:S(2)}) copy-start(bf16[1,768,1024]{2,1,0:T(8,128)(2,1)} %param.9) | copy-start | bytes 4718596
  13.9 19.1 %collective-permute-start = (bf16[96,2048]{1,0:T(8,128)(2,1)}, bf16[96,2048]{1,0:T(8,128)(2,1)S(1)}, u32[]{:S(2)}, u32[]{:S(2)}) collective-permute-start(bf16[96,2048]{1,0:T(8,128)(2,1)} %get-tuple-element.7), channel_id=1, source_target_pairs={{0,4},{4,8},{8,12},{12,16},{16,20},{20,24},{24,28},{28,32},{32,36}... | collective-permute-start | bytes 1179656 | tf_op jit(solution)/shard_map/ppermute | solution.py:22
  17.1 15.9 %collective-permute-start.1 = (bf16[96,2048]{1,0:T(8,128)(2,1)S(1)}, bf16[96,2048]{1,0:T(8,128)(2,1)S(1)}, u32[]{:S(2)}, u32[]{:S(2)}) collective-permute-start(bf16[96,2048]{1,0:T(8,128)(2,1)S(1)} %get-tuple-element.8), channel_id=1, source_target_pairs={{4,0},{8,4},{12,8},{16,12},{20,16},{24,20},{28,24},{32,28},{36,32}... | collective-permute-start | bytes 1179656 | tf_op jit(solution)/shard_map/ppermute | solution.py:25
  32.9 4.7 %copy-start.1 = (bf16[768,2048]{1,0:T(8,128)(2,1)S(1)}, bf16[768,2048]{1,0:T(8,128)(2,1)}, u32[]{:S(2)}) copy-start(bf16[768,2048]{1,0:T(8,128)(2,1)} %slice.154) | copy-start | bytes 9437188
  100.7 6.5 %copy-start.4 = (s32[4]{0:T(128)S(1)}, s32[4]{0:T(128)}, u32[]{:S(2)}) copy-start(s32[4]{0:T(128)} %param.17) | copy-start | bytes 52
  100.7 7.8 %copy-start.5 = (f32[2]{0:T(128)S(1)}, f32[2]{0:T(128)}, u32[]{:S(2)}) copy-start(f32[2]{0:T(128)} %param.16) | copy-start | bytes 28
  106.3 2.9 %collective-permute-start.2 = (bf16[384,768]{0,1:T(8,128)(2,1)}, bf16[384,768]{0,1:T(8,128)(2,1)}, u32[]{:S(2)}, u32[]{:S(2)}) collective-permute-start(bf16[384,768]{0,1:T(8,128)(2,1)} %get-tuple-element.21), channel_id=1, source_target_pairs={{0,1},{1,0},{2,3},{3,2},{4,5},{5,4},{6,7},{7,6},{8,9},{9,8},{10,11... | collective-permute-start | bytes 1769480 | tf_op jit(solution)/shard_map/ppermute | solution.py:37
  111.2 24.7 %copy-start.3 = (f32[192]{0:T(256)S(1)}, f32[192]{0:T(256)}, u32[]{:S(2)}) copy-start(f32[192]{0:T(256)} %param.15) | copy-start | bytes 2308
  111.2 11.0 %collective-permute-start.3 = (bf16[384,1]{0,1:T(2,128)(2,1)S(1)}, bf16[384,1]{0,1:T(2,128)(2,1)S(1)}, u32[]{:S(2)}, u32[]{:S(2)}) collective-permute-start(bf16[384,1]{0,1:T(2,128)(2,1)S(1)} %get-tuple-element.12), channel_id=1, source_target_pairs={{0,4},{4,8},{8,12},{12,16},{16,20},{20,24},{24,28},{28,32},{32,36}... | collective-permute-start | bytes 2312 | tf_op jit(solution)/shard_map/ppermute | solution.py:22
  113.1 11.5 %collective-permute-start.4 = (bf16[384,1]{0,1:T(2,128)(2,1)S(1)}, bf16[384,1]{0,1:T(2,128)(2,1)S(1)}, u32[]{:S(2)}, u32[]{:S(2)}) collective-permute-start(bf16[384,1]{0,1:T(2,128)(2,1)S(1)} %get-tuple-element.13), channel_id=1, source_target_pairs={{4,0},{8,4},{12,8},{16,12},{20,16},{24,20},{28,24},{32,28},{36,32}... | collective-permute-start | bytes 2312 | tf_op jit(solution)/shard_map/ppermute | solution.py:25
  126.4 9.6 %collective-permute-start.5 = (bf16[96,5]{0,1:T(8,128)(2,1)S(1)}, bf16[96,5]{0,1:T(8,128)(2,1)S(1)}, u32[]{:S(2)}, u32[]{:S(2)}) collective-permute-start(bf16[96,5]{0,1:T(8,128)(2,1)S(1)} %get-tuple-element.15), channel_id=1, source_target_pairs={{0,4},{4,8},{8,12},{12,16},{16,20},{20,24},{24,28},{28,32},{32,36}... | collective-permute-start | bytes 2888 | tf_op jit(solution)/shard_map/ppermute | solution.py:22
  128.3 8.3 %collective-permute-start.6 = (bf16[96,5]{0,1:T(8,128)(2,1)S(1)}, bf16[96,5]{0,1:T(8,128)(2,1)S(1)}, u32[]{:S(2)}, u32[]{:S(2)}) collective-permute-start(bf16[96,5]{0,1:T(8,128)(2,1)S(1)} %get-tuple-element.14), channel_id=1, source_target_pairs={{4,0},{8,4},{12,8},{16,12},{20,16},{24,20},{28,24},{32,28},{36,32}... | collective-permute-start | bytes 2888 | tf_op jit(solution)/shard_map/ppermute | solution.py:25
where the time goes:
time: 149 us; the launch traced here: 146 us
  local copies, waits for them, and re-layouts  49.1 us (33%)
  matrix products  36.4 us (24%)
  starting transfers between devices  30.7 us (21%)
  other arithmetic  28.5 us (19%)
    ppermute x3, starting transfers between devices, padded(): lax.ppermute(lax.slice_in_dim(block, 0, width, axis=dim), axis, backward)  22.7 us
    slice x2, local copies, waits for them, and re-layouts, block_attend(): key_rows[:, :, :model_width]  16.3 us
    dot_general x1, matrix products, block_attend(): jnp.einsum('nhqk,nkhd->nqhd', weights, value_heads, preferred_element_typ...  11.5 us
    slice x1, local copies, waits for them, and re-layouts, block_attend(): key_rows[:, :, model_width:]  11.1 us
    dot_general x1, matrix products, on_device(): jnp.dot(normed, project_in, preferred_element_type=jnp.float32)  8.42 us
    ppermute x3, starting transfers between devices, padded(): lax.ppermute(lax.slice_in_dim(block, block.shape[dim] - width, None, axis...  7.03 us
    sub x1, other arithmetic, block_attend(): raised = jnp.exp(scores - row_max)  6.89 us
    dot_general x1, matrix products, block_attend(): jnp.einsum('nqhd,nkhd->nhqk', query_blocks, key_heads, preferred_element_...  6.14 us
  transfers between devices with their start and end apart: 7, of which 1 were waited for; matrix products, arithmetic and copies ran while one was open for 9% of the time, Pallas kernels for 0%

commit v1 on v0

v1 whole, which is shorter than its diff:
```python
import functools
import math

import jax
import jax.numpy as jnp
from jax import lax
from jax.experimental import pallas as pl
from jax.experimental.pallas import tpu as pltpu
from jax.sharding import PartitionSpec as P

HEADS = 16
BLOCK = 48
HALF_BAND = (3.0 / 256.0, -25.0 / 256.0, 150.0 / 256.0, 150.0 / 256.0, -25.0 / 256.0, 3.0 / 256.0)
LOW_PASS = (0.012, -0.06, 0.3, 0.3, -0.06, 0.012)
CENTER_TAP = 0.5
SIN2 = (9.869604202977849, -32.469663586217976, 42.72706432039706,
        -30.100639734504547, 13.048356860034854, -3.3563323291898937)
MASKED = -1e30
MESH = pl.DeviceIdType.MESH
F32 = jnp.float32
BF16 = jnp.bfloat16

PAIR = 2 * BLOCK
LEFT = 2 * BLOCK
RIM = 16


def nt_dot(a, b):
    return lax.dot_general(a, b, (((1,), (1,)), ((), ())), preferred_element_type=F32)


def dot(a, b):
    return jnp.dot(a, b, preferred_element_type=F32)


def kernel(n_tm, hidden, modulation, w_in_hbm, w_out_hbm, w_voc_hbm, taps_hbm, alpha_hbm,
           guidance, branch_ids, out,
           hid, normed, w_in, w_out, w_voc, taps, mod, alpha,
           q_buf, k_buf, v_buf, att, upd, own, par, guided, y_buf, wave, taps_t, perm,
           win_sem, in_sem, send_sem, recv_sem):
    frames = hidden.shape[1]
    width = hidden.shape[2]
    pairs = frames // PAIR
    groups = width // 128
    extent = LEFT + frames + BLOCK
    half = out.shape[0]
    lanes = own.shape[0]
    cin = own.shape[1]
    total_frames = n_tm * frames

    tm = lax.axis_index("tm")
    member = lax.axis_index("guide")
    parity = lax.rem(member, 2)
    other = member + 1 - 2 * parity
    right_tm = lax.rem(tm + 1, n_tm)
    left_tm = lax.rem(tm + n_tm - 1, n_tm)
    left, right = (left_tm, member), (right_tm, member)
    partner = (tm, other)
    left_partner, right_partner = (left_tm, other), (right_tm, other)

    def load(src, dst, sem):
        copy = pltpu.make_async_copy(src, dst, sem)
        copy.start()
        return copy

    hid_copy = load(hidden.at[0], hid.at[pl.ds(LEFT, frames)], in_sem.at[0])
    mod_copy = load(modulation.at[:, 0], mod, in_sem.at[1])
    tiles = w_in.shape[0]
    win_copies = [load(w_in_hbm.at[:, pl.ds(256 * j, 256)], w_in.at[j], win_sem.at[j])
                  for j in range(tiles)]
    taps_copy = load(taps_hbm, taps, in_sem.at[2])
    alpha_copy = load(alpha_hbm, alpha, in_sem.at[3])
    wout_copy = load(w_out_hbm, w_out, in_sem.at[4])
    wvoc_copy = load(w_voc_hbm, w_voc, in_sem.at[5])

    barrier = pltpu.get_barrier_semaphore()
    for device in (left, right, partner, left_partner, right_partner):
        pl.semaphore_signal(barrier, inc=1, device_id=device, device_id_type=MESH)

    def send(i, src, dst, device):
        copy = pltpu.make_async_remote_copy(
            src_ref=src, dst_ref=dst, send_sem=send_sem.at[i], recv_sem=recv_sem.at[i],
            device_id=device, device_id_type=MESH)
        copy.start()
        return copy

    pl.semaphore_wait(barrier, 5)
    to_right = send(0, hidden.at[0, pl.ds(frames - LEFT, LEFT)], hid.at[pl.ds(0, LEFT)], right)
    to_left = send(1, hidden.at[0, pl.ds(0, BLOCK)], hid.at[pl.ds(LEFT + frames, BLOCK)], left)

    spare = k_buf.shape[1] - extent
    k_buf[:, pl.ds(extent, spare), :] = jnp.zeros((groups, spare, 128), BF16)
    v_buf[:, pl.ds(extent, spare), :] = jnp.zeros((groups, spare, 128), BF16)
    gap = lanes - frames - 2 * RIM
    own[pl.ds(frames + RIM, gap), :] = jnp.zeros((gap, cin), BF16)
    par[pl.ds(frames + RIM, gap), :] = jnp.zeros((gap, cin), BF16)
    row = lax.broadcasted_iota(jnp.int32, (256, 256), 0)
    col = lax.broadcasted_iota(jnp.int32, (256, 256), 1)
    perm[...] = jnp.where(row == (col % 2) * 128 + col // 2, 1.0, 0.0).astype(BF16)

    mod_copy.wait()
    scale_row = 1.0 + mod[0:1, :]
    shift_row = mod[1:2, :]

    def normalise(start, rows):
        x = hid[pl.ds(start, rows), :].astype(F32)
        centered = x - jnp.mean(x, axis=-1, keepdims=True)
        variance = jnp.mean(centered * centered, axis=-1, keepdims=True)
        result = centered * lax.rsqrt(variance + 1e-6) * scale_row + shift_row
        normed[pl.ds(start, rows), :] = result.astype(BF16)

    hid_copy.wait()

    def norm_step(i, carry):
        normalise(pl.multiple_of(LEFT + i * BLOCK, BLOCK), BLOCK)
        return carry

    lax.fori_loop(0, frames // BLOCK, norm_step, 0)

    per = groups // 2
    local = pl.ds(LEFT, frames)

    def q_step(j, carry):
        pltpu.make_async_copy(w_in.at[j], w_in.at[j], win_sem.at[j]).wait()
        acc = dot(normed[local, :], w_in[j]) * (math.log2(math.e) / math.sqrt(width // HEADS))
        acc = acc.astype(BF16)
        q_buf[2 * j] = acc[:, :128]
        q_buf[2 * j + 1] = acc[:, 128:]
        return carry

    lax.fori_loop(0, per, q_step, 0)

    def kv_local(base, buf):
        def step(j, carry):
            pltpu.make_async_copy(w_in.at[base + j], w_in.at[base + j], win_sem.at[base + j]).wait()
            acc = dot(normed[local, :], w_in[base + j]).astype(BF16)
            buf[2 * j, local, :] = acc[:, :128]
            buf[2 * j + 1, local, :] = acc[:, 128:]
            return carry
        lax.fori_loop(0, per, step, 0)

    kv_local(per, k_buf)
    kv_local(2 * per, v_buf)

    to_right.wait()
    to_left.wait()
    normalise(0, BLOCK)
    normalise(BLOCK, BLOCK)
    normalise(LEFT + frames, BLOCK)

    def kv_halo(base, buf):
        def step(j, carry):
            rows = jnp.concatenate(
                [normed[pl.ds(0, LEFT), :], normed[pl.ds(LEFT + frames, BLOCK), :]], axis=0)
            acc = dot(rows, w_in[base + j]).astype(BF16)
            for side in range(2):
                part = acc[:, 128 * side : 128 * side + 128]
                buf[2 * j + side, pl.ds(0, LEFT), :] = part[:LEFT]
                buf[2 * j + side, pl.ds(LEFT + frames, BLOCK), :] = part[LEFT:]
            return carry
        lax.fori_loop(0, per, step, 0)

    kv_halo(per, k_buf)
    kv_halo(2 * per, v_buf)

    span = 256
    lane = lax.broadcasted_iota(jnp.int32, (2 * PAIR, 128), 1)
    q_row = lax.broadcasted_iota(jnp.int32, (2 * PAIR, 128), 0)
    later = (q_row // BLOCK) % 2
    indicator = jnp.where(lane == later, 1.0, 0.0).astype(BF16)
    low_half = lax.broadcasted_iota(jnp.int32, (PAIR, 128), 1) < 64
    ones = jnp.ones((span, 128), BF16)
    key_at = lax.broadcasted_iota(jnp.int32, (span, 128), 0)
    class_at = lax.broadcasted_iota(jnp.int32, (span, 128), 1)
    window = (key_at >= class_at * BLOCK) & (key_at < class_at * BLOCK + 4 * BLOCK)

    def attend(i, first):
        p = lax.rem(first + i, pairs)
        start = pl.multiple_of(p * PAIR, PAIR)
        key_frame = tm * frames + p * PAIR - LEFT + key_at
        usable = window & (key_frame >= 0) & (key_frame < total_frames)
        bias = jnp.where(usable | (class_at > 1), 0.0, MASKED).astype(BF16)
        for g in range(groups):
            q = q_buf[g, pl.ds(start, PAIR), :]
            zero = jnp.zeros_like(q)
            q = jnp.concatenate([jnp.where(low_half, q, zero), jnp.where(low_half, zero, q)], axis=0)
            q = jnp.concatenate([q, indicator], axis=1)
            k = jnp.concatenate([k_buf[g, pl.ds(start, span), :], bias], axis=1)
            scores = nt_dot(q, k)
            raised = jnp.exp2(scores - jnp.max(scores, axis=1, keepdims=True)).astype(BF16)
            v = jnp.concatenate([v_buf[g, pl.ds(start, span), :], ones], axis=1)
            result = dot(raised, v)
            numer = jnp.where(low_half, result[:PAIR, :128], result[PAIR:, :128])
            denom = jnp.where(low_half, result[:PAIR, 128:], result[PAIR:, 128:])
            att[pl.ds(start, PAIR), pl.ds(128 * g, 128)] = (numer / denom).astype(BF16)
        return first

    gate_row = mod[2:3, :]

    def project(starts, rows):
        def rows_of(ref, offset=0):
            return jnp.concatenate([ref[pl.ds(s + offset, rows), :] for s in starts], axis=0)
        for c in range(width // 256):
            cols = pl.ds(256 * c, 256)
            mixed = dot(rows_of(att), w_out[:, cols])
            held = jnp.concatenate(
                [hid[pl.ds(LEFT + s, rows), cols] for s in starts], axis=0).astype(F32)
            upd[:, cols] = (held + gate_row[:, 256 * c : 256 * c + 256] * mixed).astype(BF16)
        result = dot(upd[...], w_voc[...]).astype(BF16)
        for at, s in enumerate(starts):
            own[pl.ds(s, rows), :] = result[at * rows : (at + 1) * rows]

    quarter = frames // 4
    lax.fori_loop(0, pairs // 2, attend, 3 * pairs // 4)
    wout_copy.wait()
    wvoc_copy.wait()
    project((3 * quarter, 0), quarter)
    last, first = pl.ds(frames - RIM, RIM), pl.ds(0, RIM)
    before, after = pl.ds(lanes - RIM, RIM), pl.ds(frames, RIM)
    sent = [
        send(2, own.at[last], own.at[before], right),
        send(3, own.at[last], par.at[before], right_partner),
        send(4, own.at[first], own.at[after], left),
        send(5, own.at[first], par.at[after], left_partner),
    ]
    for i, s in ((6, 3 * quarter), (7, 0)):
        sent.append(send(i, own.at[pl.ds(s, quarter)], par.at[pl.ds(s, quarter)], partner))
    lax.fori_loop(0, pairs // 2, attend, pairs // 4)
    project((quarter,), 2 * quarter)
    middle = pl.ds(quarter, 2 * quarter)
    sent.append(send(8, own.at[middle], par.at[middle], partner))

    taps_copy.wait()
    alpha_copy.wait()
    pick_row = lax.broadcasted_iota(jnp.int32, (half, 2 * half), 0)
    pick_col = lax.broadcasted_iota(jnp.int32, (half, 2 * half), 1)
    picked = pick_col == pick_row + parity * half
    for k in range(4):
        taps_t[pl.ds(k * half, half), :] = taps[k, pl.ds(pl.multiple_of(parity * half, half), half), :]
    rate = jnp.sum(jnp.where(picked, alpha[...], 0.0), axis=1, keepdims=True)

    for copy in sent:
        copy.wait()

    own_is_cond = branch_ids[member] == 0
    strength = guidance[member // 2]
    own_weight = jnp.where(own_is_cond, strength, 1.0 - strength)
    par_weight = jnp.where(own_is_cond, 1.0 - strength, strength)
    frame_row = lax.broadcasted_iota(jnp.int32, (lanes, 1), 0)
    frame_row = jnp.where(frame_row < frames + 2 * RIM, frame_row, frame_row - lanes) + tm * frames
    inside = (frame_row >= 0) & (frame_row < total_frames)
    mixed = own_weight * own[...].astype(F32) + par_weight * par[...].astype(F32)
    guided[...] = jnp.where(inside, mixed, 0.0).astype(BF16)

    y_buf[...] = nt_dot(taps_t[...], guided[...])

    frame_lane = lax.broadcasted_iota(jnp.int32, (8, lanes), 1)
    frame_lane = jnp.where(frame_lane < frames + 2 * RIM, frame_lane, frame_lane - lanes) + tm * frames
    kept = (frame_lane >= 0) & (frame_lane < total_frames)

    def ahead(x, count):
        return pltpu.roll(x, (-count) % lanes, 1)

    for c in range(half // 8):
        rate_c = rate[8 * c : 8 * c + 8]
        turn = rate_c * (1.0 / math.pi)
        inverse = 1.0 / rate_c

        def snake(z):
            t = turn * z
            f = t - jnp.round(t)
            u = f * f
            s = SIN2[5]
            for a in (4, 3, 2, 1, 0):
                s = s * u + SIN2[a]
            return z + (s * u) * inverse

        y = [y_buf[pl.ds(k * half + 8 * c, 8), :] for k in range(4)]
        even = jnp.where(kept, y[1] + ahead(y[3], -1), 0.0)
        odd = jnp.where(kept, ahead(y[0], 1) + y[2], 0.0)
        even_p, odd_m = ahead(even, 1), ahead(odd, -1)
        b0, b1, b2, b3, b4, b5 = HALF_BAND
        between_even = (b0 * ahead(even, -1) + b1 * odd_m + b2 * even + b3 * odd
                        + b4 * even_p + b5 * ahead(odd, 1))
        between_odd = (b0 * odd_m + b1 * even + b2 * odd + b3 * even_p
                       + b4 * ahead(odd, 1) + b5 * ahead(even, 2))
        s_even = jnp.where(kept, snake(between_even), 0.0)
        s_odd = jnp.where(kept, snake(between_odd), 0.0)
        l0, l1, l2, l3, l4, l5 = LOW_PASS
        s_even_m, s_odd_m = ahead(s_even, -1), ahead(s_odd, -1)
        s_even_p, s_odd_p = ahead(s_even, 1), ahead(s_odd, 1)
        w_even = (CENTER_TAP * snake(even) + l0 * ahead(s_odd, -2) + l1 * s_even_m + l2 * s_odd_m
                  + l3 * s_even + l4 * s_odd + l5 * s_even_p)
        w_odd = (CENTER_TAP * snake(odd) + l0 * s_even_m + l1 * s_odd_m + l2 * s_even
                 + l3 * s_odd + l4 * s_even_p + l5 * s_odd_p)
        for b in range(frames // 128):
            wave[pl.ds(8 * c, 8), pl.ds(256 * b, 128)] = w_even[:, 128 * b : 128 * b + 128]
            wave[pl.ds(8 * c, 8), pl.ds(256 * b + 128, 128)] = w_odd[:, 128 * b : 128 * b + 128]

    for b in range(frames // 128):
        cols = pl.ds(256 * b, 256)
        out[:, cols] = dot(wave[:, cols].astype(BF16), perm[...]).astype(BF16)


def on_device(hidden_rows, modulation, project_in, project_out, to_vocoder, upsample_taps,
              snake_alpha, guidance, branch_ids):
    n_tm = lax.axis_size("tm")
    _, frames, width = hidden_rows.shape
    cin, cout = upsample_taps.shape[1:]
    half = cout // 2
    extent = LEFT + frames + BLOCK
    held = (frames // PAIR - 1) * PAIR + 256
    groups = width // 128
    lanes = -(-(frames + 2 * RIM) // 128) * 128
    any_spec = pl.BlockSpec(memory_space=pl.ANY)
    smem = pl.BlockSpec(memory_space=pltpu.SMEM)
    return pl.pallas_call(
        functools.partial(kernel, n_tm),
        out_shape=jax.ShapeDtypeStruct((half, 2 * frames), BF16),
        in_specs=[any_spec] * 7 + [smem] * 2,
        out_specs=pl.BlockSpec(memory_space=pltpu.VMEM),
        scratch_shapes=[
            pltpu.VMEM((extent, width), BF16),
            pltpu.VMEM((extent, width), BF16),
            pltpu.VMEM((3 * width // 256, width, 256), BF16),
            pltpu.VMEM((width, width), BF16),
            pltpu.VMEM((width, cin), BF16),
            pltpu.VMEM((4, cout, cin), BF16),
            pltpu.VMEM((3, width), F32),
            pltpu.VMEM((1, cout), F32),
            pltpu.VMEM((groups, frames, 128), BF16),
            pltpu.VMEM((groups, held, 128), BF16),
            pltpu.VMEM((groups, held, 128), BF16),
            pltpu.VMEM((frames, width), BF16),
            pltpu.VMEM((frames // 2, width), BF16),
            pltpu.VMEM((lanes, cin), BF16),
            pltpu.VMEM((lanes, cin), BF16),
            pltpu.VMEM((lanes, cin), BF16),
            pltpu.VMEM((4 * half, lanes), F32),
            pltpu.VMEM((half, 2 * frames), F32),
            pltpu.VMEM((4 * half, cin), BF16),
            pltpu.VMEM((256, 256), BF16),
            pltpu.SemaphoreType.DMA((3 * width // 256,)),
            pltpu.SemaphoreType.DMA((6,)),
            pltpu.SemaphoreType.DMA((9,)),
            pltpu.SemaphoreType.DMA((9,)),
        ],
        compiler_params=pltpu.CompilerParams(
            collective_id=0, has_side_effects=True, vmem_limit_bytes=56 * 1024 * 1024),
        cost_estimate=pl.CostEstimate(
            flops=9_000_000_000, bytes_accessed=12_000_000, transcendentals=3_000_000),
    )(hidden_rows, modulation.transpose(1, 0, 2), project_in, project_out, to_vocoder,
      upsample_taps.transpose(0, 2, 1), snake_alpha[None, :], guidance, branch_ids)


def solution(mesh):
    in_specs = (P("guide", "tm", None), P("guide", None, None), P(), P(), P(), P(), P(), P(), P())
    return jax.shard_map(
        on_device, mesh=mesh, in_specs=in_specs, out_specs=P("guide", "tm"), check_vma=False)
```

time: 149 us -> 48.7 us (0.33)
  the two profiles are of different devices: /device:TPU:7 before, /device:TPU:1 now
where the time goes in v1:
time: 48.7 us; the launch traced here: 48.5 us
  Pallas kernels  46.8 us (96%)
  local copies, waits for them, and re-layouts  1.69 us (3%)
    pallas_call x1, Pallas kernels, on_device(): pl.pallas_call(functools.partial(kernel, n_tm), out_shape=jax.ShapeDtypeS...  46.8 us
    unnamed x1, local copies, waits for them, and re-layouts  1.69 us

profile of v1, /device:TPU:1, one launch (start us, length us, event | category | flops | bytes accessed | tf_op | source)
XLA Modules:
  0.0 48.5 jit_solution(11233168942883563238)
XLA Ops:
  0.0 46.8 %shard_map.91 = bf16[96,1536]{1,0:T(8,128)(2,1)} custom-call(bf16[1,768,1024]{2,1,0:T(8,128)(2,1)} %hidden.1, f32[3,1,1024]{2,1,0:T(1,128)} %bitcast.4, bf16[1024,3072]{1,0:T(8,128)(2,1)} %w_in_hbm.1, bf16[1024,1024]{1,0:T(8,128)(2,1)} %w_out_hbm.1, bf16[1024,384]{1,0:T(8,128)(2,1)} %w_voc_hbm.1, bf16[4,192,384]{2,1,0:T(8,128)(2,1)} %bitcast.3, ...), custom_call_target="tpu_custom_call" | custom-call | flops 8999999488 | bytes 12000000 | tf_op jit(solution)/shard_map/pallas_call | solution.py:317
  46.8 1.7 %copy.11 = bf16[96,1536]{1,0:T(8,128)(2,1)} copy(bf16[96,1536]{1,0:T(8,128)(2,1)} %shard_map.91) | data formatting | bytes 589824

commit v2 on v1

--- a/solution.py
+++ b/solution.py
@@ -37,7 +37,7 @@
            guidance, branch_ids, out,
            hid, normed, w_in, w_out, w_voc, taps, mod, alpha,
            q_buf, k_buf, v_buf, att, upd, own, par, guided, y_buf, wave, taps_t, perm,
-           win_sem, in_sem, send_sem, recv_sem):
+           hid_sem, win_sem, in_sem, send_sem, recv_sem):
     frames = hidden.shape[1]
     width = hidden.shape[2]
     pairs = frames // PAIR
@@ -63,15 +63,11 @@
         copy.start()
         return copy
 
-    hid_copy = load(hidden.at[0], hid.at[pl.ds(LEFT, frames)], in_sem.at[0])
-    mod_copy = load(modulation.at[:, 0], mod, in_sem.at[1])
-    tiles = w_in.shape[0]
-    win_copies = [load(w_in_hbm.at[:, pl.ds(256 * j, 256)], w_in.at[j], win_sem.at[j])
-                  for j in range(tiles)]
-    taps_copy = load(taps_hbm, taps, in_sem.at[2])
-    alpha_copy = load(alpha_hbm, alpha, in_sem.at[3])
-    wout_copy = load(w_out_hbm, w_out, in_sem.at[4])
-    wvoc_copy = load(w_voc_hbm, w_voc, in_sem.at[5])
+    parts = 4
+    part = frames // parts
+    hid_copies = [load(hidden.at[0, pl.ds(part * i, part)], hid.at[pl.ds(LEFT + part * i, part)],
+                       hid_sem.at[i]) for i in range(parts)]
+    mod_copy = load(modulation.at[:, 0], mod, in_sem.at[0])
 
     barrier = pltpu.get_barrier_semaphore()
     for device in (left, right, partner, left_partner, right_partner):
@@ -84,6 +80,17 @@
         copy.start()
         return copy
 
+    def load_weights():
+        tiles = w_in.shape[0]
+        copies = [load(w_in_hbm.at[:, pl.ds(256 * j, 256)], w_in.at[j], win_sem.at[j])
+                  for j in range(tiles)]
+        for i, (src, dst) in enumerate(((w_out_hbm, w_out), (w_voc_hbm, w_voc),
+                                        (taps_hbm, taps), (alpha_hbm, alpha))):
+            copies.append(load(src, dst, in_sem.at[i + 1]))
+        return copies[tiles:]
+
+    hid_copies[0].wait()
+    wout_copy, wvoc_copy, taps_copy, alpha_copy = load_weights()
     pl.semaphore_wait(barrier, 5)
     to_right = send(0, hidden.at[0, pl.ds(frames - LEFT, LEFT)], hid.at[pl.ds(0, LEFT)], right)
     to_left = send(1, hidden.at[0, pl.ds(0, BLOCK)], hid.at[pl.ds(LEFT + frames, BLOCK)], left)
@@ -109,13 +116,15 @@
         result = centered * lax.rsqrt(variance + 1e-6) * scale_row + shift_row
         normed[pl.ds(start, rows), :] = result.astype(BF16)
 
-    hid_copy.wait()
-
-    def norm_step(i, carry):
-        normalise(pl.multiple_of(LEFT + i * BLOCK, BLOCK), BLOCK)
-        return carry
-
-    lax.fori_loop(0, frames // BLOCK, norm_step, 0)
+    for i in range(parts):
+        if i > 0:
+            hid_copies[i].wait()
+
+        def norm_step(j, carry):
+            normalise(pl.multiple_of(LEFT + i * part + j * PAIR, PAIR), PAIR)
+            return carry
+
+        lax.fori_loop(0, part // PAIR, norm_step, 0)
 
     per = groups // 2
     local = pl.ds(LEFT, frames)
@@ -130,70 +139,68 @@
 
     lax.fori_loop(0, per, q_step, 0)
 
-    def kv_local(base, buf):
+    def keys_values(base, buf):
         def step(j, carry):
             pltpu.make_async_copy(w_in.at[base + j], w_in.at[base + j], win_sem.at[base + j]).wait()
-            acc = dot(normed[local, :], w_in[base + j]).astype(BF16)
-            buf[2 * j, local, :] = acc[:, :128]
-            buf[2 * j + 1, local, :] = acc[:, 128:]
+            acc = dot(normed[...], w_in[base + j]).astype(BF16)
+            buf[2 * j, pl.ds(0, extent), :] = acc[:, :128]
+            buf[2 * j + 1, pl.ds(0, extent), :] = acc[:, 128:]
             return carry
         lax.fori_loop(0, per, step, 0)
 
-    kv_local(per, k_buf)
-    kv_local(2 * per, v_buf)
-
     to_right.wait()
     to_left.wait()
-    normalise(0, BLOCK)
-    normalise(BLOCK, BLOCK)
+    normalise(0, LEFT)
     normalise(LEFT + frames, BLOCK)
-
-    def kv_halo(base, buf):
-        def step(j, carry):
-            rows = jnp.concatenate(
-                [normed[pl.ds(0, LEFT), :], normed[pl.ds(LEFT + frames, BLOCK), :]], axis=0)
-            acc = dot(rows, w_in[base + j]).astype(BF16)
-            for side in range(2):
-                part = acc[:, 128 * side : 128 * side + 128]
-                buf[2 * j + side, pl.ds(0, LEFT), :] = part[:LEFT]
-                buf[2 * j + side, pl.ds(LEFT + frames, BLOCK), :] = part[LEFT:]
-            return carry
-        lax.fori_loop(0, per, step, 0)
-
-    kv_halo(per, k_buf)
-    kv_halo(2 * per, v_buf)
+    keys_values(per, k_buf)
+    keys_values(2 * per, v_buf)
 
     span = 256
-    lane = lax.broadcasted_iota(jnp.int32, (2 * PAIR, 128), 1)
-    q_row = lax.broadcasted_iota(jnp.int32, (2 * PAIR, 128), 0)
-    later = (q_row // BLOCK) % 2
-    indicator = jnp.where(lane == later, 1.0, 0.0).astype(BF16)
     low_half = lax.broadcasted_iota(jnp.int32, (PAIR, 128), 1) < 64
     ones = jnp.ones((span, 128), BF16)
-    key_at = lax.broadcasted_iota(jnp.int32, (span, 128), 0)
-    class_at = lax.broadcasted_iota(jnp.int32, (span, 128), 1)
-    window = (key_at >= class_at * BLOCK) & (key_at < class_at * BLOCK + 4 * BLOCK)
-
-    def attend(i, first):
-        p = lax.rem(first + i, pairs)
-        start = pl.multiple_of(p * PAIR, PAIR)
-        key_frame = tm * frames + p * PAIR - LEFT + key_at
-        usable = window & (key_frame >= 0) & (key_frame < total_frames)
-        bias = jnp.where(usable | (class_at > 1), 0.0, MASKED).astype(BF16)
-        for g in range(groups):
-            q = q_buf[g, pl.ds(start, PAIR), :]
+    key_at = lax.broadcasted_iota(jnp.int32, (PAIR, span), 1)
+    block_at = lax.broadcasted_iota(jnp.int32, (PAIR, span), 0) // BLOCK * BLOCK
+    window = (key_at >= block_at) & (key_at < block_at + 4 * BLOCK)
+
+    def bias_of(p):
+        usable = window
+        if p == 0:
+            usable = usable & ((key_at >= LEFT) | (tm > 0))
+        if p == pairs - 1:
+            usable = usable & ((key_at < LEFT + PAIR) | (tm < n_tm - 1))
+        return jnp.where(usable, 0.0, MASKED)
+
+    def attend(members):
+        biases = {p: bias_of(p) for p in members}
+        steps = [(p, g) for p in members for g in range(groups)]
+        scores, raised = {}, {}
+
+        def score(step):
+            p, g = step
+            q = q_buf[g, pl.ds(p * PAIR, PAIR), :]
             zero = jnp.zeros_like(q)
             q = jnp.concatenate([jnp.where(low_half, q, zero), jnp.where(low_half, zero, q)], axis=0)
-            q = jnp.concatenate([q, indicator], axis=1)
-            k = jnp.concatenate([k_buf[g, pl.ds(start, span), :], bias], axis=1)
-            scores = nt_dot(q, k)
-            raised = jnp.exp2(scores - jnp.max(scores, axis=1, keepdims=True)).astype(BF16)
-            v = jnp.concatenate([v_buf[g, pl.ds(start, span), :], ones], axis=1)
-            result = dot(raised, v)
+            s = dot(q, jnp.transpose(k_buf[g, pl.ds(p * PAIR, span), :]))
+            return jnp.concatenate([s[:PAIR] + biases[p], s[PAIR:] + biases[p]], axis=0)
+
+        def raise_to(s):
+            return jnp.exp2(s - jnp.max(s, axis=1, keepdims=True)).astype(BF16)
+
+        def combine(step, weights):
+            p, g = step
+            v = jnp.concatenate([v_buf[g, pl.ds(p * PAIR, span), :], ones], axis=1)
+            result = dot(weights, v)
             numer = jnp.where(low_half, result[:PAIR, :128], result[PAIR:, :128])
             denom = jnp.where(low_half, result[:PAIR, 128:], result[PAIR:, 128:])
-            att[pl.ds(start, PAIR), pl.ds(128 * g, 128)] = (numer / denom).astype(BF16)
-        return first
+            att[pl.ds(p * PAIR, PAIR), pl.ds(128 * g, 128)] = (numer / denom).astype(BF16)
+
+        for t in range(len(steps) + 2):
+            if t < len(steps):
+                scores[t] = score(steps[t])
+            if 0 <= t - 1 < len(steps):
+                raised[t - 1] = raise_to(scores.pop(t - 1))
+            if t >= 2:
+                combine(steps[t - 2], raised.pop(t - 2))
 
     gate_row = mod[2:3, :]
 
@@ -211,7 +218,7 @@
             own[pl.ds(s, rows), :] = result[at * rows : (at + 1) * rows]
 
     quarter = frames // 4
-    lax.fori_loop(0, pairs // 2, attend, 3 * pairs // 4)
+    attend([(3 * pairs // 4 + i) % pairs for i in range(pairs // 2)])
     wout_copy.wait()
     wvoc_copy.wait()
     project((3 * quarter, 0), quarter)
@@ -225,7 +232,7 @@
     ]
     for i, s in ((6, 3 * quarter), (7, 0)):
         sent.append(send(i, own.at[pl.ds(s, quarter)], par.at[pl.ds(s, quarter)], partner))
-    lax.fori_loop(0, pairs // 2, attend, pairs // 4)
+    attend([pairs // 4 + i for i in range(pairs // 2)])
     project((quarter,), 2 * quarter)
     middle = pl.ds(quarter, 2 * quarter)
     sent.append(send(8, own.at[middle], par.at[middle], partner))
@@ -340,8 +347,9 @@
             pltpu.VMEM((half, 2 * frames), F32),
             pltpu.VMEM((4 * half, cin), BF16),
             pltpu.VMEM((256, 256), BF16),
+            pltpu.SemaphoreType.DMA((4,)),
             pltpu.SemaphoreType.DMA((3 * width // 256,)),
-            pltpu.SemaphoreType.DMA((6,)),
+            pltpu.SemaphoreType.DMA((5,)),
             pltpu.SemaphoreType.DMA((9,)),
             pltpu.SemaphoreType.DMA((9,)),
         ],

time: 48.7 us -> 34.6 us (0.71)
  Pallas kernels: 46.8 us -> 32.7 us
    pallas_call x1, Pallas kernels: 46.8 us -> 32.7 us  [on_device(): pl.pallas_call(functools.partial(kernel, n_tm), out_shape=jax.ShapeDtypeS...]
where the time goes in v2:
time: 34.6 us; the launch traced here: 34.4 us
  Pallas kernels  32.7 us (95%)
  local copies, waits for them, and re-layouts  1.69 us (5%)
    pallas_call x1, Pallas kernels, on_device(): pl.pallas_call(functools.partial(kernel, n_tm), out_shape=jax.ShapeDtypeS...  32.7 us
    unnamed x1, local copies, waits for them, and re-layouts  1.69 us

profile of v2, /device:TPU:1, one launch (start us, length us, event | category | flops | bytes accessed | tf_op | source)
XLA Modules:
  0.0 34.4 jit_solution(1450143660577968487)
XLA Ops:
  0.0 32.7 %shard_map.91 = bf16[96,1536]{1,0:T(8,128)(2,1)} custom-call(bf16[1,768,1024]{2,1,0:T(8,128)(2,1)} %hidden.1, f32[3,1,1024]{2,1,0:T(1,128)} %bitcast.4, bf16[1024,3072]{1,0:T(8,128)(2,1)} %w_in_hbm.1, bf16[1024,1024]{1,0:T(8,128)(2,1)} %w_out_hbm.1, bf16[1024,384]{1,0:T(8,128)(2,1)} %w_voc_hbm.1, bf16[4,192,384]{2,1,0:T(8,128)(2,1)} %bitcast.3, ...), custom_call_target="tpu_custom_call" | custom-call | flops 8999999488 | bytes 12000000 | tf_op jit(solution)/shard_map/pallas_call | solution.py:324
  32.7 1.7 %copy.11 = bf16[96,1536]{1,0:T(8,128)(2,1)} copy(bf16[96,1536]{1,0:T(8,128)(2,1)} %shard_map.91) | data formatting | bytes 589824

commit v3 on v2

--- a/solution.py
+++ b/solution.py
@@ -52,8 +52,10 @@
     member = lax.axis_index("guide")
     parity = lax.rem(member, 2)
     other = member + 1 - 2 * parity
-    right_tm = lax.rem(tm + 1, n_tm)
-    left_tm = lax.rem(tm + n_tm - 1, n_tm)
+    has_left, has_right = tm > 0, tm < n_tm - 1
+    late = tm == n_tm // 2
+    prompt = jnp.logical_not(late)
+    left_tm, right_tm = jnp.maximum(tm - 1, 0), jnp.minimum(tm + 1, n_tm - 1)
     left, right = (left_tm, member), (right_tm, member)
     partner = (tm, other)
     left_partner, right_partner = (left_tm, other), (right_tm, other)
@@ -70,15 +72,29 @@
     mod_copy = load(modulation.at[:, 0], mod, in_sem.at[0])
 
     barrier = pltpu.get_barrier_semaphore()
-    for device in (left, right, partner, left_partner, right_partner):
-        pl.semaphore_signal(barrier, inc=1, device_id=device, device_id_type=MESH)
-
-    def send(i, src, dst, device):
-        copy = pltpu.make_async_remote_copy(
+
+    def greet(*devices):
+        for device in devices:
+            pl.semaphore_signal(barrier, inc=1, device_id=device, device_id_type=MESH)
+
+    greet(partner)
+    pl.when(has_left)(lambda: greet(left, left_partner))
+    pl.when(has_right)(lambda: greet(right, right_partner))
+
+    def transfer(i, src, dst, device):
+        return pltpu.make_async_remote_copy(
             src_ref=src, dst_ref=dst, send_sem=send_sem.at[i], recv_sem=recv_sem.at[i],
             device_id=device, device_id_type=MESH)
-        copy.start()
-        return copy
+
+    def start(*copies):
+        for copy in copies:
+            copy.start()
+
+    def wait(sent, received):
+        for copy in sent:
+            copy.wait_send()
+        for copy in received:
+            copy.wait_recv()
 
     def load_weights():
         tiles = w_in.shape[0]
@@ -91,16 +107,37 @@
 
     hid_copies[0].wait()
     wout_copy, wvoc_copy, taps_copy, alpha_copy = load_weights()
-    pl.semaphore_wait(barrier, 5)
-    to_right = send(0, hidden.at[0, pl.ds(frames - LEFT, LEFT)], hid.at[pl.ds(0, LEFT)], right)
-    to_left = send(1, hidden.at[0, pl.ds(0, BLOCK)], hid.at[pl.ds(LEFT + frames, BLOCK)], left)
+
+    to_right = transfer(0, hidden.at[0, pl.ds(frames - LEFT, LEFT)], hid.at[pl.ds(0, LEFT)], right)
+    to_left = transfer(1, hidden.at[0, pl.ds(0, BLOCK)], hid.at[pl.ds(LEFT + frames, BLOCK)], left)
+
+    def share_hidden():
+        pl.semaphore_wait(
+            barrier, 1 + 2 * has_left.astype(jnp.int32) + 2 * has_right.astype(jnp.int32))
+        pl.when(has_right)(lambda: start(to_right))
+        pl.when(has_left)(lambda: start(to_left))
 
     spare = k_buf.shape[1] - extent
     k_buf[:, pl.ds(extent, spare), :] = jnp.zeros((groups, spare, 128), BF16)
     v_buf[:, pl.ds(extent, spare), :] = jnp.zeros((groups, spare, 128), BF16)
     gap = lanes - frames - 2 * RIM
-    own[pl.ds(frames + RIM, gap), :] = jnp.zeros((gap, cin), BF16)
-    par[pl.ds(frames + RIM, gap), :] = jnp.zeros((gap, cin), BF16)
+
+    def clear(start, count):
+        own[pl.ds(start, count), :] = jnp.zeros((count, cin), BF16)
+        par[pl.ds(start, count), :] = jnp.zeros((count, cin), BF16)
+
+    clear(frames + RIM, gap)
+
+    @pl.when(tm == 0)
+    def _():
+        hid[pl.ds(0, LEFT), :] = jnp.zeros((LEFT, width), BF16)
+        clear(lanes - RIM, RIM)
+
+    @pl.when(tm == n_tm - 1)
+    def _():
+        hid[pl.ds(LEFT + frames, BLOCK), :] = jnp.zeros((BLOCK, width), BF16)
+        clear(frames, RIM)
+
     row = lax.broadcasted_iota(jnp.int32, (256, 256), 0)
     col = lax.broadcasted_iota(jnp.int32, (256, 256), 1)
     perm[...] = jnp.where(row == (col % 2) * 128 + col // 2, 1.0, 0.0).astype(BF16)
@@ -125,6 +162,8 @@
             return carry
 
         lax.fori_loop(0, part // PAIR, norm_step, 0)
+        if i == 1:
+            pl.when(prompt)(share_hidden)
 
     per = groups // 2
     local = pl.ds(LEFT, frames)
@@ -139,19 +178,17 @@
 
     lax.fori_loop(0, per, q_step, 0)
 
+    pl.when(late)(share_hidden)
+
     def keys_values(base, buf):
         def step(j, carry):
             pltpu.make_async_copy(w_in.at[base + j], w_in.at[base + j], win_sem.at[base + j]).wait()
-            acc = dot(normed[...], w_in[base + j]).astype(BF16)
-            buf[2 * j, pl.ds(0, extent), :] = acc[:, :128]
-            buf[2 * j + 1, pl.ds(0, extent), :] = acc[:, 128:]
+            acc = dot(normed[local, :], w_in[base + j]).astype(BF16)
+            buf[2 * j, local, :] = acc[:, :128]
+            buf[2 * j + 1, local, :] = acc[:, 128:]
             return carry
         lax.fori_loop(0, per, step, 0)
 
-    to_right.wait()
-    to_left.wait()
-    normalise(0, LEFT)
-    normalise(LEFT + frames, BLOCK)
     keys_values(per, k_buf)
     keys_values(2 * per, v_buf)
 
@@ -218,24 +255,52 @@
             own[pl.ds(s, rows), :] = result[at * rows : (at + 1) * rows]
 
     quarter = frames // 4
-    attend([(3 * pairs // 4 + i) % pairs for i in range(pairs // 2)])
+    last, first = pl.ds(frames - RIM, RIM), pl.ds(0, RIM)
+    before, after = pl.ds(lanes - RIM, RIM), pl.ds(frames, RIM)
+    rightward = (transfer(2, own.at[last], own.at[before], right),
+                 transfer(3, own.at[last], par.at[before], right_partner))
+    leftward = (transfer(4, own.at[first], own.at[after], left),
+                transfer(5, own.at[first], par.at[after], left_partner))
+    shared = [transfer(i, own.at[pl.ds(s, n)], par.at[pl.ds(s, n)], partner)
+              for i, s, n in ((6, 3 * quarter, quarter), (7, 0, quarter), (8, quarter, 2 * quarter))]
+
     wout_copy.wait()
     wvoc_copy.wait()
+
+    def inner_half():
+        attend([pairs // 4 + i for i in range(pairs // 2)])
+        project((quarter,), 2 * quarter)
+        start(shared[2])
+
+    pl.when(late)(inner_half)
+
+    pl.when(has_left)(lambda: wait((to_left,), (to_right,)))
+    pl.when(has_right)(lambda: wait((to_right,), (to_left,)))
+    normalise(0, LEFT)
+    normalise(LEFT + frames, BLOCK)
+    rim_rows = jnp.concatenate(
+        [normed[pl.ds(0, LEFT), :], normed[pl.ds(LEFT + frames, BLOCK), :]], axis=0)
+
+    def rim_keys_values(base, buf):
+        def step(j, carry):
+            acc = dot(rim_rows, w_in[base + j]).astype(BF16)
+            for side in range(2):
+                part = acc[:, 128 * side : 128 * side + 128]
+                buf[2 * j + side, pl.ds(0, LEFT), :] = part[:LEFT]
+                buf[2 * j + side, pl.ds(LEFT + frames, BLOCK), :] = part[LEFT:]
+            return carry
+        lax.fori_loop(0, per, step, 0)
+
+    rim_keys_values(per, k_buf)
+    rim_keys_values(2 * per, v_buf)
+
+    attend([(3 * pairs // 4 + i) % pairs for i in range(pairs // 2)])
     project((3 * quarter, 0), quarter)
-    last, first = pl.ds(frames - RIM, RIM), pl.ds(0, RIM)
-    before, after = pl.ds(lanes - RIM, RIM), pl.ds(frames, RIM)
-    sent = [
-        send(2, own.at[last], own.at[before], right),
-        send(3, own.at[last], par.at[before], right_partner),
-        send(4, own.at[first], own.at[after], left),
-        send(5, own.at[first], par.at[after], left_partner),
-    ]
-    for i, s in ((6, 3 * quarter), (7, 0)):
-        sent.append(send(i, own.at[pl.ds(s, quarter)], par.at[pl.ds(s, quarter)], partner))
-    attend([pairs // 4 + i for i in range(pairs // 2)])
-    project((quarter,), 2 * quarter)
-    middle = pl.ds(quarter, 2 * quarter)
-    sent.append(send(8, own.at[middle], par.at[middle], partner))
+    pl.when(has_right)(lambda: start(*rightward))
+    pl.when(has_left)(lambda: start(*leftward))
+    start(*shared[:2])
+
+    pl.when(prompt)(inner_half)
 
     taps_copy.wait()
     alpha_copy.wait()
@@ -246,8 +311,9 @@
         taps_t[pl.ds(k * half, half), :] = taps[k, pl.ds(pl.multiple_of(parity * half, half), half), :]
     rate = jnp.sum(jnp.where(picked, alpha[...], 0.0), axis=1, keepdims=True)
 
-    for copy in sent:
-        copy.wait()
+    pl.when(has_right)(lambda: wait(rightward, leftward))
+    pl.when(has_left)(lambda: wait(leftward, rightward))
+    wait(shared, shared)
 
     own_is_cond = branch_ids[member] == 0
     strength = guidance[member // 2]

time: 34.6 us -> 30.1 us (0.87)
  the two profiles are of different devices: /device:TPU:1 before, /device:TPU:7 now
where the time goes in v3:
time: 30.1 us; the launch traced here: 29.9 us
  Pallas kernels  28.2 us (94%)
  local copies, waits for them, and re-layouts  1.69 us (6%)
    pallas_call x1, Pallas kernels, on_device(): pl.pallas_call(functools.partial(kernel, n_tm), out_shape=jax.ShapeDtypeS...  28.2 us
    unnamed x1, local copies, waits for them, and re-layouts  1.69 us

profile of v3, /device:TPU:7, one launch (start us, length us, event | category | flops | bytes accessed | tf_op | source)
XLA Modules:
  0.0 29.9 jit_solution(9745809096246504317)
XLA Ops:
  0.0 28.2 %shard_map.91 = bf16[96,1536]{1,0:T(8,128)(2,1)} custom-call(bf16[1,768,1024]{2,1,0:T(8,128)(2,1)} %hidden.1, f32[3,1,1024]{2,1,0:T(1,128)} %bitcast.4, bf16[1024,3072]{1,0:T(8,128)(2,1)} %w_in_hbm.1, bf16[1024,1024]{1,0:T(8,128)(2,1)} %w_out_hbm.1, bf16[1024,384]{1,0:T(8,128)(2,1)} %w_voc_hbm.1, bf16[4,192,384]{2,1,0:T(8,128)(2,1)} %bitcast.3, ...), custom_call_target="tpu_custom_call" | custom-call | flops 8999999488 | bytes 12000000 | tf_op jit(solution)/shard_map/pallas_call | solution.py:390
  28.2 1.7 %copy.11 = bf16[96,1536]{1,0:T(8,128)(2,1)} copy(bf16[96,1536]{1,0:T(8,128)(2,1)} %shard_map.91) | data formatting | bytes 589824

commit v4 on v3

--- a/solution.py
+++ b/solution.py
@@ -168,26 +168,25 @@
     per = groups // 2
     local = pl.ds(LEFT, frames)
 
-    def q_step(j, carry):
-        pltpu.make_async_copy(w_in.at[j], w_in.at[j], win_sem.at[j]).wait()
+    def arrived(base):
+        for j in range(base, base + per):
+            pltpu.make_async_copy(w_in.at[j], w_in.at[j], win_sem.at[j]).wait()
+
+    arrived(0)
+    for j in range(per):
         acc = dot(normed[local, :], w_in[j]) * (math.log2(math.e) / math.sqrt(width // HEADS))
         acc = acc.astype(BF16)
         q_buf[2 * j] = acc[:, :128]
         q_buf[2 * j + 1] = acc[:, 128:]
-        return carry
-
-    lax.fori_loop(0, per, q_step, 0)
 
     pl.when(late)(share_hidden)
 
     def keys_values(base, buf):
-        def step(j, carry):
-            pltpu.make_async_copy(w_in.at[base + j], w_in.at[base + j], win_sem.at[base + j]).wait()
+        arrived(base)
+        for j in range(per):
             acc = dot(normed[local, :], w_in[base + j]).astype(BF16)
             buf[2 * j, local, :] = acc[:, :128]
             buf[2 * j + 1, local, :] = acc[:, 128:]
-            return carry
-        lax.fori_loop(0, per, step, 0)
 
     keys_values(per, k_buf)
     keys_values(2 * per, v_buf)
@@ -282,14 +281,12 @@
         [normed[pl.ds(0, LEFT), :], normed[pl.ds(LEFT + frames, BLOCK), :]], axis=0)
 
     def rim_keys_values(base, buf):
-        def step(j, carry):
+        for j in range(per):
             acc = dot(rim_rows, w_in[base + j]).astype(BF16)
             for side in range(2):
                 part = acc[:, 128 * side : 128 * side + 128]
                 buf[2 * j + side, pl.ds(0, LEFT), :] = part[:LEFT]
                 buf[2 * j + side, pl.ds(LEFT + frames, BLOCK), :] = part[LEFT:]
-            return carry
-        lax.fori_loop(0, per, step, 0)
 
     rim_keys_values(per, k_buf)
     rim_keys_values(2 * per, v_buf)
@@ -389,7 +386,7 @@
     smem = pl.BlockSpec(memory_space=pltpu.SMEM)
     return pl.pallas_call(
         functools.partial(kernel, n_tm),
-        out_shape=jax.ShapeDtypeStruct((half, 2 * frames), BF16),
+        out_shape=pltpu.VMEM((half, 2 * frames), BF16),
         in_specs=[any_spec] * 7 + [smem] * 2,
         out_specs=pl.BlockSpec(memory_space=pltpu.VMEM),
         scratch_shapes=[

time: 30.1 us -> 26.5 us (0.88)
  Pallas kernels: 28.2 us -> 25.6 us
  local copies, waits for them, and re-layouts: 1.69 us -> 0.72 us
    pallas_call x1, Pallas kernels: 28.2 us -> 25.6 us  [on_device(): pl.pallas_call(functools.partial(kernel, n_tm), out_shape=pltpu.VMEM((hal...]
    unnamed x1, local copies, waits for them, and re-layouts: 1.69 us -> 0.72 us
where the time goes in v4:
time: 26.5 us; the launch traced here: 26.4 us
  Pallas kernels  25.6 us (97%)
  local copies, waits for them, and re-layouts  0.72 us (3%)
    pallas_call x1, Pallas kernels, on_device(): pl.pallas_call(functools.partial(kernel, n_tm), out_shape=pltpu.VMEM((hal...  25.6 us
    unnamed x1, local copies, waits for them, and re-layouts  0.72 us

profile of v4, /device:TPU:7, one launch (start us, length us, event | category | flops | bytes accessed | tf_op | source)
XLA Modules:
  0.0 26.4 jit_solution(10318727633449123494)
XLA Ops:
  0.0 25.6 %shard_map.91 = bf16[96,1536]{1,0:T(8,128)(2,1)S(1)} custom-call(bf16[1,768,1024]{2,1,0:T(8,128)(2,1)} %hidden.1, f32[3,1,1024]{2,1,0:T(1,128)} %bitcast.4, bf16[1024,3072]{1,0:T(8,128)(2,1)} %w_in_hbm.1, bf16[1024,1024]{1,0:T(8,128)(2,1)} %w_out_hbm.1, bf16[1024,384]{1,0:T(8,128)(2,1)} %w_voc_hbm.1, bf16[4,192,384]{2,1,0:T(8,128)(2,1)} %bitcast.3, ...), custom_call_target="tpu_custom_call" | custom-call | flops 8999999488 | bytes 12000000 | tf_op jit(solution)/shard_map/pallas_call | solution.py:387
  25.7 0.7 %copy.11 = bf16[96,1536]{1,0:T(8,128)(2,1)} copy(bf16[96,1536]{1,0:T(8,128)(2,1)S(1)} %shard_map.91) | data formatting | bytes 589824

commit v5 on v4

--- a/solution.py
+++ b/solution.py
@@ -22,6 +22,7 @@
 
 PAIR = 2 * BLOCK
 LEFT = 2 * BLOCK
+RING = 4
 RIM = 16
 
 
@@ -53,12 +54,26 @@
     parity = lax.rem(member, 2)
     other = member + 1 - 2 * parity
     has_left, has_right = tm > 0, tm < n_tm - 1
-    late = tm == n_tm // 2
+    deferred = tm == n_tm // 2
+    late = deferred | (tm == n_tm // 2 + 1)
     prompt = jnp.logical_not(late)
+    split = deferred | (tm == n_tm // 2 - 1)
+    whole = jnp.logical_not(split)
+    eager = lax.rem(tm, RING) == RING - 1
     left_tm, right_tm = jnp.maximum(tm - 1, 0), jnp.minimum(tm + 1, n_tm - 1)
     left, right = (left_tm, member), (right_tm, member)
     partner = (tm, other)
     left_partner, right_partner = (left_tm, other), (right_tm, other)
+
+    barrier = pltpu.get_barrier_semaphore()
+
+    def greet(*devices):
+        for device in devices:
+            pl.semaphore_signal(barrier, inc=1, device_id=device, device_id_type=MESH)
+
+    greet(partner)
+    pl.when(has_left)(lambda: greet(left, left_partner))
+    pl.when(has_right)(lambda: greet(right, right_partner))
 
     def load(src, dst, sem):
         copy = pltpu.make_async_copy(src, dst, sem)
@@ -71,16 +86,6 @@
                        hid_sem.at[i]) for i in range(parts)]
     mod_copy = load(modulation.at[:, 0], mod, in_sem.at[0])
 
-    barrier = pltpu.get_barrier_semaphore()
-
-    def greet(*devices):
-        for device in devices:
-            pl.semaphore_signal(barrier, inc=1, device_id=device, device_id_type=MESH)
-
-    greet(partner)
-    pl.when(has_left)(lambda: greet(left, left_partner))
-    pl.when(has_right)(lambda: greet(right, right_partner))
-
     def transfer(i, src, dst, device):
         return pltpu.make_async_remote_copy(
             src_ref=src, dst_ref=dst, send_sem=send_sem.at[i], recv_sem=recv_sem.at[i],
@@ -95,6 +100,17 @@
             copy.wait_send()
         for copy in received:
             copy.wait_recv()
+
+    to_right = transfer(0, hidden.at[0, pl.ds(frames - LEFT, LEFT)], hid.at[pl.ds(0, LEFT)], right)
+    to_left = transfer(1, hidden.at[0, pl.ds(0, BLOCK)], hid.at[pl.ds(LEFT + frames, BLOCK)], left)
+
+    def share_hidden():
+        pl.semaphore_wait(
+            barrier, 1 + 2 * has_left.astype(jnp.int32) + 2 * has_right.astype(jnp.int32))
+        pl.when(has_right)(lambda: start(to_right))
+        pl.when(has_left)(lambda: start(to_left))
+
+    pl.when(eager)(share_hidden)
 
     def load_weights():
         tiles = w_in.shape[0]
@@ -108,15 +124,6 @@
     hid_copies[0].wait()
     wout_copy, wvoc_copy, taps_copy, alpha_copy = load_weights()
 
-    to_right = transfer(0, hidden.at[0, pl.ds(frames - LEFT, LEFT)], hid.at[pl.ds(0, LEFT)], right)
-    to_left = transfer(1, hidden.at[0, pl.ds(0, BLOCK)], hid.at[pl.ds(LEFT + frames, BLOCK)], left)
-
-    def share_hidden():
-        pl.semaphore_wait(
-            barrier, 1 + 2 * has_left.astype(jnp.int32) + 2 * has_right.astype(jnp.int32))
-        pl.when(has_right)(lambda: start(to_right))
-        pl.when(has_left)(lambda: start(to_left))
-
     spare = k_buf.shape[1] - extent
     k_buf[:, pl.ds(extent, spare), :] = jnp.zeros((groups, spare, 128), BF16)
     v_buf[:, pl.ds(extent, spare), :] = jnp.zeros((groups, spare, 128), BF16)
@@ -163,7 +170,7 @@
 
         lax.fori_loop(0, part // PAIR, norm_step, 0)
         if i == 1:
-            pl.when(prompt)(share_hidden)
+            pl.when(jnp.logical_not(deferred | eager))(share_hidden)
 
     per = groups // 2
     local = pl.ds(LEFT, frames)
@@ -179,17 +186,18 @@
         q_buf[2 * j] = acc[:, :128]
         q_buf[2 * j + 1] = acc[:, 128:]
 
-    pl.when(late)(share_hidden)
-
-    def keys_values(base, buf):
-        arrived(base)
-        for j in range(per):
+    def keys_values(base, buf, tiles):
+        for j in tiles:
             acc = dot(normed[local, :], w_in[base + j]).astype(BF16)
             buf[2 * j, local, :] = acc[:, :128]
             buf[2 * j + 1, local, :] = acc[:, 128:]
 
-    keys_values(per, k_buf)
-    keys_values(2 * per, v_buf)
+    arrived(per)
+    arrived(2 * per)
+    keys_values(per, k_buf, range(per))
+    keys_values(2 * per, v_buf, range(per // 2))
+    pl.when(deferred)(share_hidden)
+    keys_values(2 * per, v_buf, range(per // 2, per))
 
     span = 256
     low_half = lax.broadcasted_iota(jnp.int32, (PAIR, 128), 1) < 64
@@ -241,6 +249,7 @@
     gate_row = mod[2:3, :]
 
     def project(starts, rows):
+        count = rows * len(starts)
         def rows_of(ref, offset=0):
             return jnp.concatenate([ref[pl.ds(s + offset, rows), :] for s in starts], axis=0)
         for c in range(width // 256):
@@ -248,8 +257,8 @@
             mixed = dot(rows_of(att), w_out[:, cols])
             held = jnp.concatenate(
                 [hid[pl.ds(LEFT + s, rows), cols] for s in starts], axis=0).astype(F32)
-            upd[:, cols] = (held + gate_row[:, 256 * c : 256 * c + 256] * mixed).astype(BF16)
-        result = dot(upd[...], w_voc[...]).astype(BF16)
+            upd[pl.ds(0, count), cols] = (held + gate_row[:, 256 * c : 256 * c + 256] * mixed).astype(BF16)
+        result = dot(upd[pl.ds(0, count), :], w_voc[...]).astype(BF16)
         for at, s in enumerate(starts):
             own[pl.ds(s, rows), :] = result[at * rows : (at + 1) * rows]
 
@@ -261,17 +270,17 @@
     leftward = (transfer(4, own.at[first], own.at[after], left),
                 transfer(5, own.at[first], par.at[after], left_partner))
     shared = [transfer(i, own.at[pl.ds(s, n)], par.at[pl.ds(s, n)], partner)
-              for i, s, n in ((6, 3 * quarter, quarter), (7, 0, quarter), (8, quarter, 2 * quarter))]
+              for i, s, n in ((6, 3 * quarter, quarter), (7, 0, quarter), (8, quarter, 2 * quarter),
+                              (6, PAIR, frames - 2 * PAIR), (7, frames - PAIR, PAIR), (8, 0, PAIR))]
 
     wout_copy.wait()
     wvoc_copy.wait()
 
-    def inner_half():
-        attend([pairs // 4 + i for i in range(pairs // 2)])
-        project((quarter,), 2 * quarter)
-        start(shared[2])
-
-    pl.when(late)(inner_half)
+    @pl.when(late)
+    def _():
+        attend([i for i in range(1, pairs - 1)])
+        project((PAIR,), frames - 2 * PAIR)
+        start(shared[3])
 
     pl.when(has_left)(lambda: wait((to_left,), (to_right,)))
     pl.when(has_right)(lambda: wait((to_right,), (to_left,)))
@@ -291,13 +300,26 @@
     rim_keys_values(per, k_buf)
     rim_keys_values(2 * per, v_buf)
 
-    attend([(3 * pairs // 4 + i) % pairs for i in range(pairs // 2)])
-    project((3 * quarter, 0), quarter)
-    pl.when(has_right)(lambda: start(*rightward))
-    pl.when(has_left)(lambda: start(*leftward))
-    start(*shared[:2])
-
-    pl.when(prompt)(inner_half)
+    def send_rims():
+        pl.when(has_right)(lambda: start(*rightward))
+        pl.when(has_left)(lambda: start(*leftward))
+
+    @pl.when(late)
+    def _():
+        attend([pairs - 1, 0])
+        project((frames - PAIR, 0), PAIR)
+        send_rims()
+        start(*shared[4:])
+
+    @pl.when(prompt)
+    def _():
+        attend([(3 * pairs // 4 + i) % pairs for i in range(pairs // 2)])
+        project((3 * quarter, 0), quarter)
+        send_rims()
+        start(*shared[:2])
+        attend([pairs // 4 + i for i in range(pairs // 2)])
+        project((quarter,), 2 * quarter)
+        start(shared[2])
 
     taps_copy.wait()
     alpha_copy.wait()
@@ -308,68 +330,96 @@
         taps_t[pl.ds(k * half, half), :] = taps[k, pl.ds(pl.multiple_of(parity * half, half), half), :]
     rate = jnp.sum(jnp.where(picked, alpha[...], 0.0), axis=1, keepdims=True)
 
-    pl.when(has_right)(lambda: wait(rightward, leftward))
-    pl.when(has_left)(lambda: wait(leftward, rightward))
-    wait(shared, shared)
+    def rims_arrived():
+        pl.when(has_right)(lambda: wait(rightward, leftward))
+        pl.when(has_left)(lambda: wait(leftward, rightward))
+
+    pl.when(prompt)(lambda: wait(shared[:3], shared[:3]))
+    pl.when(late)(lambda: wait(shared[3:], shared[3:]))
 
     own_is_cond = branch_ids[member] == 0
     strength = guidance[member // 2]
     own_weight = jnp.where(own_is_cond, strength, 1.0 - strength)
     par_weight = jnp.where(own_is_cond, 1.0 - strength, strength)
-    frame_row = lax.broadcasted_iota(jnp.int32, (lanes, 1), 0)
-    frame_row = jnp.where(frame_row < frames + 2 * RIM, frame_row, frame_row - lanes) + tm * frames
-    inside = (frame_row >= 0) & (frame_row < total_frames)
-    mixed = own_weight * own[...].astype(F32) + par_weight * par[...].astype(F32)
-    guided[...] = jnp.where(inside, mixed, 0.0).astype(BF16)
-
-    y_buf[...] = nt_dot(taps_t[...], guided[...])
-
-    frame_lane = lax.broadcasted_iota(jnp.int32, (8, lanes), 1)
-    frame_lane = jnp.where(frame_lane < frames + 2 * RIM, frame_lane, frame_lane - lanes) + tm * frames
-    kept = (frame_lane >= 0) & (frame_lane < total_frames)
-
-    def ahead(x, count):
-        return pltpu.roll(x, (-count) % lanes, 1)
-
-    for c in range(half // 8):
-        rate_c = rate[8 * c : 8 * c + 8]
-        turn = rate_c * (1.0 / math.pi)
-        inverse = 1.0 / rate_c
-
-        def snake(z):
-            t = turn * z
-            f = t - jnp.round(t)
-            u = f * f
-            s = SIN2[5]
-            for a in (4, 3, 2, 1, 0):
-                s = s * u + SIN2[a]
-            return z + (s * u) * inverse
-
-        y = [y_buf[pl.ds(k * half + 8 * c, 8), :] for k in range(4)]
-        even = jnp.where(kept, y[1] + ahead(y[3], -1), 0.0)
-        odd = jnp.where(kept, ahead(y[0], 1) + y[2], 0.0)
-        even_p, odd_m = ahead(even, 1), ahead(odd, -1)
-        b0, b1, b2, b3, b4, b5 = HALF_BAND
-        between_even = (b0 * ahead(even, -1) + b1 * odd_m + b2 * even + b3 * odd
-                        + b4 * even_p + b5 * ahead(odd, 1))
-        between_odd = (b0 * odd_m + b1 * even + b2 * odd + b3 * even_p
-                       + b4 * ahead(odd, 1) + b5 * ahead(even, 2))
-        s_even = jnp.where(kept, snake(between_even), 0.0)
-        s_odd = jnp.where(kept, snake(between_odd), 0.0)
-        l0, l1, l2, l3, l4, l5 = LOW_PASS
-        s_even_m, s_odd_m = ahead(s_even, -1), ahead(s_odd, -1)
-        s_even_p, s_odd_p = ahead(s_even, 1), ahead(s_odd, 1)
-        w_even = (CENTER_TAP * snake(even) + l0 * ahead(s_odd, -2) + l1 * s_even_m + l2 * s_odd_m
-                  + l3 * s_even + l4 * s_odd + l5 * s_even_p)
-        w_odd = (CENTER_TAP * snake(odd) + l0 * s_even_m + l1 * s_odd_m + l2 * s_even
-                 + l3 * s_odd + l4 * s_even_p + l5 * s_odd_p)
-        for b in range(frames // 128):
-            wave[pl.ds(8 * c, 8), pl.ds(256 * b, 128)] = w_even[:, 128 * b : 128 * b + 128]
-            wave[pl.ds(8 * c, 8), pl.ds(256 * b + 128, 128)] = w_odd[:, 128 * b : 128 * b + 128]
-
-    for b in range(frames // 128):
-        cols = pl.ds(256 * b, 256)
-        out[:, cols] = dot(wave[:, cols].astype(BF16), perm[...]).astype(BF16)
+    def frame_of(at):
+        return jnp.where(at < frames + 2 * RIM, at, at - lanes) + tm * frames
+
+    def mix(start, rows):
+        frame = frame_of(lax.broadcasted_iota(jnp.int32, (rows, 1), 0) + start)
+        inside = (frame >= 0) & (frame < total_frames)
+        part = pl.ds(start, rows)
+        mixed = own_weight * own[part, :].astype(F32) + par_weight * par[part, :].astype(F32)
+        guided[part, :] = jnp.where(inside, mixed, 0.0).astype(BF16)
+        y_buf[:, part] = nt_dot(taps_t[...], guided[part, :])
+
+    def finish(tiles, results):
+        extent_lanes = 128 * len(tiles)
+        lane_at = lax.broadcasted_iota(jnp.int32, (8, 128), 1)
+        frame_lane = frame_of(jnp.concatenate([lane_at + 128 * t for t in tiles], axis=1))
+        kept = (frame_lane >= 0) & (frame_lane < total_frames)
+
+        def ahead(x, count):
+            return pltpu.roll(x, (-count) % extent_lanes, 1)
+
+        for c in range(half // 8):
+            rate_c = rate[8 * c : 8 * c + 8]
+            turn = rate_c * (1.0 / math.pi)
+            inverse = 1.0 / rate_c
+
+            def snake(z):
+                t = turn * z
+                f = t - jnp.round(t)
+                u = f * f
+                s = SIN2[5]
+                for a in (4, 3, 2, 1, 0):
+                    s = s * u + SIN2[a]
+                return z + (s * u) * inverse
+
+            y = [jnp.concatenate([y_buf[pl.ds(k * half + 8 * c, 8), pl.ds(128 * t, 128)] for t in tiles],
+                                 axis=1) for k in range(4)]
+            even = jnp.where(kept, y[1] + ahead(y[3], -1), 0.0)
+            odd = jnp.where(kept, ahead(y[0], 1) + y[2], 0.0)
+            even_p, odd_m = ahead(even, 1), ahead(odd, -1)
+            b0, b1, b2, b3, b4, b5 = HALF_BAND
+            between_even = (b0 * ahead(even, -1) + b1 * odd_m + b2 * even + b3 * odd
+                            + b4 * even_p + b5 * ahead(odd, 1))
+            between_odd = (b0 * odd_m + b1 * even + b2 * odd + b3 * even_p
+                           + b4 * ahead(odd, 1) + b5 * ahead(even, 2))
+            s_even = jnp.where(kept, snake(between_even), 0.0)
+            s_odd = jnp.where(kept, snake(between_odd), 0.0)
+            l0, l1, l2, l3, l4, l5 = LOW_PASS
+            s_even_m, s_odd_m = ahead(s_even, -1), ahead(s_odd, -1)
+            s_even_p, s_odd_p = ahead(s_even, 1), ahead(s_odd, 1)
+            w_even = (CENTER_TAP * snake(even) + l0 * ahead(s_odd, -2) + l1 * s_even_m + l2 * s_odd_m
+                      + l3 * s_even + l4 * s_odd + l5 * s_even_p)
+            w_odd = (CENTER_TAP * snake(odd) + l0 * s_even_m + l1 * s_odd_m + l2 * s_even
+                     + l3 * s_odd + l4 * s_even_p + l5 * s_odd_p)
+            for b in results:
+                at = 128 * tiles.index(b)
+                wave[pl.ds(8 * c, 8), pl.ds(256 * b, 128)] = w_even[:, at : at + 128]
+                wave[pl.ds(8 * c, 8), pl.ds(256 * b + 128, 128)] = w_odd[:, at : at + 128]
+
+        for b in results:
+            cols = pl.ds(256 * b, 256)
+            out[:, cols] = dot(wave[:, cols].astype(BF16), perm[...]).astype(BF16)
+
+
+    n_tiles = lanes // 128
+    out_tiles = frames // 128
+
+    @pl.when(whole)
+    def _():
+        rims_arrived()
+        mix(0, lanes)
+        finish(list(range(n_tiles)), list(range(out_tiles)))
+
+    @pl.when(split)
+    def _():
+        mix(0, frames)
+        finish(list(range(out_tiles)), list(range(1, out_tiles - 1)))
+        rims_arrived()
+        mix(frames, lanes - frames)
+        finish(list(range(out_tiles - 2, n_tiles)) + [0, 1], [out_tiles - 1, 0])
 
 
 def on_device(hidden_rows, modulation, project_in, project_out, to_vocoder, upsample_taps,
@@ -402,7 +452,7 @@
             pltpu.VMEM((groups, held, 128), BF16),
             pltpu.VMEM((groups, held, 128), BF16),
             pltpu.VMEM((frames, width), BF16),
-            pltpu.VMEM((frames // 2, width), BF16),
+            pltpu.VMEM((frames, width), BF16),
             pltpu.VMEM((lanes, cin), BF16),
             pltpu.VMEM((lanes, cin), BF16),
             pltpu.VMEM((lanes, cin), BF16),

time: 26.5 us -> 26.6 us (level)
  no operation moved by 1% of the time
where the time goes in v5:
time: 26.6 us; the launch traced here: 26.4 us
  Pallas kernels  25.7 us (97%)
  local copies, waits for them, and re-layouts  0.72 us (3%)
    pallas_call x1, Pallas kernels, on_device(): pl.pallas_call(functools.partial(kernel, n_tm), out_shape=pltpu.VMEM((hal...  25.7 us
    unnamed x1, local copies, waits for them, and re-layouts  0.72 us

profile of v5, /device:TPU:7, one launch (start us, length us, event | category | flops | bytes accessed | tf_op | source)
XLA Modules:
  0.0 26.4 jit_solution(9641541502265609113)
XLA Ops:
  0.0 25.7 %shard_map.91 = bf16[96,1536]{1,0:T(8,128)(2,1)S(1)} custom-call(bf16[1,768,1024]{2,1,0:T(8,128)(2,1)} %hidden.1, f32[3,1,1024]{2,1,0:T(1,128)} %bitcast.4, bf16[1024,3072]{1,0:T(8,128)(2,1)} %w_in_hbm.1, bf16[1024,1024]{1,0:T(8,128)(2,1)} %w_out_hbm.1, bf16[1024,384]{1,0:T(8,128)(2,1)} %w_voc_hbm.1, bf16[4,192,384]{2,1,0:T(8,128)(2,1)} %bitcast.3, ...), custom_call_target="tpu_custom_call" | custom-call | flops 8999999488 | bytes 12000000 | tf_op jit(solution)/shard_map/pallas_call | solution.py:437
  25.7 0.7 %copy.11 = bf16[96,1536]{1,0:T(8,128)(2,1)} copy(bf16[96,1536]{1,0:T(8,128)(2,1)S(1)} %shard_map.91) | data formatting | bytes 589824

commit v6 on v5

--- a/solution.py
+++ b/solution.py
@@ -56,8 +56,9 @@
     has_left, has_right = tm > 0, tm < n_tm - 1
     deferred = tm == n_tm // 2
     late = deferred | (tm == n_tm // 2 + 1)
-    prompt = jnp.logical_not(late)
-    split = deferred | (tm == n_tm // 2 - 1)
+    leader = tm == n_tm // 2 - 1
+    prompt = jnp.logical_not(late | leader)
+    split = deferred | leader
     whole = jnp.logical_not(split)
     eager = lax.rem(tm, RING) == RING - 1
     left_tm, right_tm = jnp.maximum(tm - 1, 0), jnp.minimum(tm + 1, n_tm - 1)
@@ -104,11 +105,14 @@
     to_right = transfer(0, hidden.at[0, pl.ds(frames - LEFT, LEFT)], hid.at[pl.ds(0, LEFT)], right)
     to_left = transfer(1, hidden.at[0, pl.ds(0, BLOCK)], hid.at[pl.ds(LEFT + frames, BLOCK)], left)
 
-    def share_hidden():
+    def share_hidden(left_first=False):
         pl.semaphore_wait(
             barrier, 1 + 2 * has_left.astype(jnp.int32) + 2 * has_right.astype(jnp.int32))
+        if left_first:
+            pl.when(has_left)(lambda: start(to_left))
         pl.when(has_right)(lambda: start(to_right))
-        pl.when(has_left)(lambda: start(to_left))
+        if not left_first:
+            pl.when(has_left)(lambda: start(to_left))
 
     pl.when(eager)(share_hidden)
 
@@ -196,7 +200,7 @@
     arrived(2 * per)
     keys_values(per, k_buf, range(per))
     keys_values(2 * per, v_buf, range(per // 2))
-    pl.when(deferred)(share_hidden)
+    pl.when(deferred)(lambda: share_hidden(True))
     keys_values(2 * per, v_buf, range(per // 2, per))
 
     span = 256
@@ -271,7 +275,8 @@
                 transfer(5, own.at[first], par.at[after], left_partner))
     shared = [transfer(i, own.at[pl.ds(s, n)], par.at[pl.ds(s, n)], partner)
               for i, s, n in ((6, 3 * quarter, quarter), (7, 0, quarter), (8, quarter, 2 * quarter),
-                              (6, PAIR, frames - 2 * PAIR), (7, frames - PAIR, PAIR), (8, 0, PAIR))]
+                              (6, PAIR, frames - 2 * PAIR), (7, frames - PAIR, PAIR), (8, 0, PAIR),
+                              (6, 0, frames - PAIR))]
 
     wout_copy.wait()
     wvoc_copy.wait()
@@ -281,6 +286,10 @@
         attend([i for i in range(1, pairs - 1)])
         project((PAIR,), frames - 2 * PAIR)
         start(shared[3])
+
+    @pl.when(leader)
+    def _():
+        attend([i for i in range(2, pairs - 2)])
 
     pl.when(has_left)(lambda: wait((to_left,), (to_right,)))
     pl.when(has_right)(lambda: wait((to_right,), (to_left,)))
@@ -309,7 +318,18 @@
         attend([pairs - 1, 0])
         project((frames - PAIR, 0), PAIR)
         send_rims()
-        start(*shared[4:])
+        start(*shared[4:6])
+
+    @pl.when(leader)
+    def _():
+        attend([pairs - 1])
+        project((frames - PAIR,), PAIR)
+        pl.when(has_right)(lambda: start(*rightward))
+        start(shared[4])
+        attend([0, 1, pairs - 2])
+        project((0,), frames - PAIR)
+        pl.when(has_left)(lambda: start(*leftward))
+        start(shared[6])
 
     @pl.when(prompt)
     def _():
@@ -335,7 +355,8 @@
         pl.when(has_left)(lambda: wait(leftward, rightward))
 
     pl.when(prompt)(lambda: wait(shared[:3], shared[:3]))
-    pl.when(late)(lambda: wait(shared[3:], shared[3:]))
+    pl.when(late)(lambda: wait(shared[3:6], shared[3:6]))
+    pl.when(leader)(lambda: wait((shared[4], shared[6]), (shared[4], shared[6])))
 
     own_is_cond = branch_ids[member] == 0
     strength = guidance[member // 2]

time: 26.6 us -> 25.1 us (0.944)
  Pallas kernels: 25.7 us -> 24.2 us
    pallas_call x1, Pallas kernels: 25.7 us -> 24.2 us  [on_device(): pl.pallas_call(functools.partial(kernel, n_tm), out_shape=pltpu.VMEM((hal...]
where the time goes in v6:
time: 25.1 us; the launch traced here: 24.9 us
  Pallas kernels  24.2 us (96%)
  local copies, waits for them, and re-layouts  0.72 us (3%)
    pallas_call x1, Pallas kernels, on_device(): pl.pallas_call(functools.partial(kernel, n_tm), out_shape=pltpu.VMEM((hal...  24.2 us
    unnamed x1, local copies, waits for them, and re-layouts  0.72 us

profile of v6, /device:TPU:7, one launch (start us, length us, event | category | flops | bytes accessed | tf_op | source)
XLA Modules:
  0.0 24.9 jit_solution(10570228280589653165)
XLA Ops:
  0.0 24.2 %shard_map.91 = bf16[96,1536]{1,0:T(8,128)(2,1)S(1)} custom-call(bf16[1,768,1024]{2,1,0:T(8,128)(2,1)} %hidden.1, f32[3,1,1024]{2,1,0:T(1,128)} %bitcast.4, bf16[1024,3072]{1,0:T(8,128)(2,1)} %w_in_hbm.1, bf16[1024,1024]{1,0:T(8,128)(2,1)} %w_out_hbm.1, bf16[1024,384]{1,0:T(8,128)(2,1)} %w_voc_hbm.1, bf16[4,192,384]{2,1,0:T(8,128)(2,1)} %bitcast.3, ...), custom_call_target="tpu_custom_call" | custom-call | flops 8999999488 | bytes 12000000 | tf_op jit(solution)/shard_map/pallas_call | solution.py:458
  24.2 0.7 %copy.11 = bf16[96,1536]{1,0:T(8,128)(2,1)} copy(bf16[96,1536]{1,0:T(8,128)(2,1)S(1)} %shard_map.91) | data formatting | bytes 589824

commit v7 on v6

--- a/solution.py
+++ b/solution.py
@@ -350,9 +350,15 @@
         taps_t[pl.ds(k * half, half), :] = taps[k, pl.ds(pl.multiple_of(parity * half, half), half), :]
     rate = jnp.sum(jnp.where(picked, alpha[...], 0.0), axis=1, keepdims=True)
 
+    def right_rim_arrived():
+        pl.when(has_right)(lambda: wait(rightward, leftward))
+
+    def left_rim_arrived():
+        pl.when(has_left)(lambda: wait(leftward, rightward))
+
     def rims_arrived():
-        pl.when(has_right)(lambda: wait(rightward, leftward))
-        pl.when(has_left)(lambda: wait(leftward, rightward))
+        right_rim_arrived()
+        left_rim_arrived()
 
     pl.when(prompt)(lambda: wait(shared[:3], shared[:3]))
     pl.when(late)(lambda: wait(shared[3:6], shared[3:6]))
@@ -434,7 +440,16 @@
         mix(0, lanes)
         finish(list(range(n_tiles)), list(range(out_tiles)))
 
-    @pl.when(split)
+    @pl.when(deferred)
+    def _():
+        right_rim_arrived()
+        mix(0, frames + RIM)
+        finish(list(range(n_tiles)), list(range(1, out_tiles)))
+        left_rim_arrived()
+        mix(frames, lanes - frames)
+        finish([n_tiles - 1, 0, 1], [0])
+
+    @pl.when(leader)
     def _():
         mix(0, frames)
         finish(list(range(out_tiles)), list(range(1, out_tiles - 1)))

time: 25.1 us -> 24.8 us (0.988)
  Pallas kernels: 24.2 us -> 23.9 us
    pallas_call x1, Pallas kernels: 24.2 us -> 23.9 us  [on_device(): pl.pallas_call(functools.partial(kernel, n_tm), out_shape=pltpu.VMEM((hal...]
where the time goes in v7:
time: 24.8 us; the launch traced here: 24.6 us
  Pallas kernels  23.9 us (96%)
  local copies, waits for them, and re-layouts  0.72 us (3%)
    pallas_call x1, Pallas kernels, on_device(): pl.pallas_call(functools.partial(kernel, n_tm), out_shape=pltpu.VMEM((hal...  23.9 us
    unnamed x1, local copies, waits for them, and re-layouts  0.72 us

profile of v7, /device:TPU:7, one launch (start us, length us, event | category | flops | bytes accessed | tf_op | source)
XLA Modules:
  0.0 24.6 jit_solution(11298470958755406340)
XLA Ops:
  0.0 23.9 %shard_map.91 = bf16[96,1536]{1,0:T(8,128)(2,1)S(1)} custom-call(bf16[1,768,1024]{2,1,0:T(8,128)(2,1)} %hidden.1, f32[3,1,1024]{2,1,0:T(1,128)} %bitcast.4, bf16[1024,3072]{1,0:T(8,128)(2,1)} %w_in_hbm.1, bf16[1024,1024]{1,0:T(8,128)(2,1)} %w_out_hbm.1, bf16[1024,384]{1,0:T(8,128)(2,1)} %w_voc_hbm.1, bf16[4,192,384]{2,1,0:T(8,128)(2,1)} %bitcast.3, ...), custom_call_target="tpu_custom_call" | custom-call | flops 8999999488 | bytes 12000000 | tf_op jit(solution)/shard_map/pallas_call | solution.py:473
  23.9 0.7 %copy.11 = bf16[96,1536]{1,0:T(8,128)(2,1)} copy(bf16[96,1536]{1,0:T(8,128)(2,1)S(1)} %shard_map.91) | data formatting | bytes 589824
